TPU v7x, 256 devices: a whole 4x4x8 slice. The times are simulated.
256 devices in a mesh: seg: 16 (over y, x), sec: 16 (over z, core).
Axes of the slice: x: 4, y: 4, z: 8, core: 2. Of those that a mesh axis runs over, the one named last changes fastest.
Arguments:
- left_env: bfloat16 [16, 400, 256, 256], P('seg', 'sec'), as said below
- right_env: bfloat16 [16, 400, 256, 256], P('seg', 'sec'), as said below
- edge_site: bfloat16 [16, 256, 256], P('seg'), may hold values from -0.375 to 0.375
- psi_one: bfloat16 [16, 256, 256], P('seg'), may hold values from -6 to 6
- psi_two: bfloat16 [16, 256, 256], P('seg'), may hold values from -6 to 6
- mpo_gain: float32 [16, 400], P('seg', 'sec'), may hold values from 0.5 to 2
- kept: int32 [16, 2], P('seg'), may hold values from 64 to 256, as said below
Outputs:
- psi_first: float32 [16, 256, 256], P('seg', 'sec')
- psi_second: float32 [16, 256, 256], P('seg', 'sec')
Inputs may be any that keep to these rules, and one draw needn't show every extreme that they name: `kept`: some entry equals 256 and some equals 64. `left_env`: every [256, 256] block is symmetric, with entries of order (26214400) ** -0.25. `right_env`: every [256, 256] block is symmetric, with entries of order (26214400) ** -0.25.
All inputs are finite; a program needn't handle non-finite values.
Results may differ from a plain program's by a relative error of at most 0.03.
Values may be sent and summed in bfloat16 or wider, within the bound.
No kernel may reach another device: no remote copies, remote signals or barrier semaphores. Data moves between devices by JAX's collectives and lax.ppermute only.
A program may use at most 64 MiB of HBM per device.

v0:
```python
import functools

import jax
import jax.numpy as jnp
from jax import lax
from jax.experimental import pallas as pl
from jax.experimental.pallas import tpu as pltpu
from jax.sharding import PartitionSpec as P

ITERS = 3
EPSILON = 1e-06
DESCENT = 0.3
CHUNK = 5
MIB = 1024 * 1024
GATHERED = True

F32 = jnp.float32
BF16 = jnp.bfloat16


def dot(a, b, dims=((1,), (0,))):
    return lax.dot_general(a, b, (dims, ((), ())), preferred_element_type=F32)


def live_rows(shape, live):
    return lax.broadcasted_iota(jnp.int32, shape, 0) < live


def begun(start, live):
    states = start.shape[-1]
    block = start[...].reshape(states, states).astype(F32)
    block = jnp.where(live_rows(block.shape, live), block, 0.0)
    return block * (states / jnp.sqrt(jnp.sum(block * block) + EPSILON))


def joined(summed, live):
    if len(summed) == 1:
        states = summed[0].shape[2]
        product = summed[0][...].reshape(states, states).astype(F32)
    else:
        low = lax.rem(lax.axis_index("sec"), 2) == 0
        own, far = summed[0][...].astype(F32), summed[1][...].astype(F32)
        product = jnp.concatenate([jnp.where(low, own, far), jnp.where(low, far, own)], axis=0)
    return jnp.where(live_rows(product.shape, live), product, 0.0)


def coefficients(current, product):
    states = current.shape[0]
    xx, xy = jnp.sum(current * current), jnp.sum(current * product)
    yy = jnp.sum(product * product)
    energy = xy / xx
    norm = xx + DESCENT * DESCENT * jnp.maximum(yy - energy * xy, 0.0)
    scale = states / jnp.sqrt(norm + EPSILON)
    return scale * (1.0 + DESCENT * energy), -DESCENT * scale


def stepped(vector, summed, live):
    current, product = vector[...], joined(summed, live)
    a, b = coefficients(current, product)
    return a * current + b * product


def own_rows(block, rows):
    share = rows.shape[1]
    rows[0] = block[pl.ds(pl.multiple_of(lax.axis_index("sec") * share, share), share), :]


def contract(vector, left, right, acc):
    states = vector.shape[0]
    terms = left.shape[0]
    chunk = CHUNK if terms % CHUNK == 0 else 1
    for first in range(0, terms, chunk):
        inner = dot(left[first : first + chunk].reshape(chunk * states, states), vector)
        total = None
        for n in range(chunk):
            part = dot(inner[n * states : (n + 1) * states].astype(BF16), right[first + n])
            total = part if total is None else total + part
        if first == 0:
            acc[...] = total
        else:
            acc[...] += total


def hand_out(acc, mine, theirs):
    half = mine.shape[0]
    core = lax.rem(lax.axis_index("sec"), 2)
    mine[...] = acc[pl.ds(pl.multiple_of(core * half, half), half), :].astype(BF16)
    theirs[...] = acc[pl.ds(pl.multiple_of((1 - core) * half, half), half), :].astype(BF16)


def first_start(kept, start, left, right, vector, mine, theirs, applied, acc):
    states = start.shape[2]
    block = jnp.where(live_rows((states, states), kept[0, 0]), start[0].astype(F32), 0.0)
    scale = states / jnp.sqrt(jnp.sum(block * block) + EPSILON)
    vector[...] = block * scale
    contract(block.astype(BF16), left.at[0], right.at[0], acc)
    applied[...] = acc[...] * scale
    hand_out(applied, mine, theirs)


def first_step(
    kept, vector, applied, summed, left, right, after, mine, theirs, applied_after, acc
):
    current, product = vector[...], joined(summed, kept[0, 0])
    a, b = coefficients(current, product)
    contract(product.astype(BF16), left.at[0], right.at[0], acc)
    after[...] = a * current + b * product
    applied_after[...] = a * applied[...] + b * acc[...]
    hand_out(applied_after, mine, theirs)


def place(shape):
    return lax.broadcasted_iota(jnp.int32, shape, 0), lax.broadcasted_iota(jnp.int32, shape, 1)


def pack(gain, left, edge, ready, package):
    terms, states = left.shape[1], left.shape[2]
    row, column = place((states, states))
    pairs = terms // 2

    def scaled(n):
        return left[0, n].astype(F32) * gain[0, n]

    for n in range(pairs):
        second = scaled(2 * n + 1)
        slab = jnp.where(row >= column, scaled(2 * n), second)
        package[n * states : (n + 1) * states] = slab.astype(BF16)
        diagonal = jnp.sum(jnp.where(row == column, second, 0.0), axis=0, keepdims=True)
        base = (pairs + terms % 2 + 1) * states + 16 * n
        package[base : base + 16] = jnp.broadcast_to(diagonal, (16, states)).astype(BF16)
    if terms % 2:
        package[pairs * states : (pairs + 1) * states] = scaled(terms - 1).astype(BF16)
    last = pairs + terms % 2
    package[last * states : (last + 1) * states] = edge[0]


def unpack(kept, gain, left, package, start, incoming, site, vector, turned):
    terms, states = left.shape[1], left.shape[2]
    row, column = place((states, states))
    pairs = terms // 2
    at_start = lax.axis_index("seg") == 0

    @pl.when(at_start)
    def _():
        for n in range(terms):
            incoming[n] = (left[0, n].astype(F32) * gain[0, n]).astype(BF16)
        site[...] = jnp.where(row == column, 1.0, 0.0).astype(BF16)

    @pl.when(jnp.logical_not(at_start))
    def _():
        for n in range(pairs):
            slab = package[n * states : (n + 1) * states].astype(F32)
            mirrored = slab.T
            base = (pairs + terms % 2 + 1) * states + 16 * n
            diagonal = package[base : base + 16].astype(F32)[0:1]
            one = jnp.where(row >= column, slab, mirrored)
            two = jnp.where(row < column, slab, jnp.where(row == column, diagonal, mirrored))
            incoming[2 * n] = (one * gain[0, 2 * n]).astype(BF16)
            incoming[2 * n + 1] = (two * gain[0, 2 * n + 1]).astype(BF16)
        if terms % 2:
            slab = package[pairs * states : (pairs + 1) * states].astype(F32)
            incoming[terms - 1] = (slab * gain[0, terms - 1]).astype(BF16)
        last = pairs + terms % 2
        site[...] = package[last * states : (last + 1) * states]

    current = begun(start, kept[0, 1])
    vector[...] = current
    turned[...] = dot(site[...], current.astype(BF16)).astype(BF16)


def second_apply(inner, edge, site, incoming, right, acc):
    contract(inner, incoming, right.at[0], acc)
    outer = dot(acc[...].astype(BF16), site, ((1,), (1,))).astype(BF16)
    return dot(edge[...], outer, ((0,), (0,)))


def second_start(
    kept, vector, summed, turned, edge, incoming, right, rows, site, mine, theirs, applied, acc
):
    states = vector.shape[1]
    acc[...] = stepped(vector, summed, kept[0, 0])
    own_rows(acc, rows)
    site_left = (acc[...] * states**-0.5).astype(BF16)
    site[...] = site_left
    inner = dot(turned[...], site_left).astype(BF16)
    applied[...] = second_apply(inner, edge, site_left, incoming, right, acc)
    hand_out(applied, mine, theirs)


def second_step(
    kept, vector, applied, summed, site, edge, incoming, right,
    after, mine, theirs, applied_after, acc,
):
    current, product = vector[...], joined(summed, kept[0, 1])
    a, b = coefficients(current, product)
    inner = dot(product.astype(BF16), site[...]).astype(BF16)
    inner = dot(edge[...], inner).astype(BF16)
    found = second_apply(inner, edge, site[...], incoming, right, acc)
    after[...] = a * current + b * product
    applied_after[...] = a * applied[...] + b * found
    hand_out(applied_after, mine, theirs)


def second_end(kept, vector, summed, rows, acc):
    acc[...] = stepped(vector, summed, kept[0, 1])
    own_rows(acc, rows)


def add(count, *refs):
    total = refs[0][...].astype(F32)
    for ref in refs[1:count]:
        total = total + ref[...].astype(F32)
    refs[-1][...] = total.astype(BF16)


def on_device(left_env, right_env, edge_site, psi_one, psi_two, mpo_gain, kept):
    terms, states = left_env.shape[1], left_env.shape[2]
    sections, segments = lax.axis_size("sec"), lax.axis_size("seg")
    share, half = states // sections, states // 2

    smem = pl.BlockSpec(memory_space=pltpu.SMEM)
    vmem = pl.BlockSpec(memory_space=pltpu.VMEM)

    def shape(*dims, dtype=BF16):
        return jax.ShapeDtypeStruct(dims, dtype)

    block = shape(states, states, dtype=F32)
    halves = [shape(half, states)] * 2
    rows = shape(1, share, states, dtype=F32)
    acc = pltpu.VMEM((states, states), F32)
    apply_cost = pl.CostEstimate(
        flops=4 * terms * states**3, bytes_accessed=4 * terms * states**2, transcendentals=0
    )

    def call(kernel, ins, outs, scratch=(acc,), limit=12 * MIB, cost=None, name=None):
        return pl.pallas_call(
            kernel,
            in_specs=ins,
            out_specs=[vmem] * len(outs),
            out_shape=outs,
            scratch_shapes=list(scratch),
            compiler_params=pltpu.CompilerParams(vmem_limit_bytes=limit),
            cost_estimate=cost,
            name=name or kernel.__name__,
        )

    def step_call(kernel, before, total, after, step):
        outs, scratch = [block, *halves], [acc]
        if step < ITERS - 2:
            outs.append(block)
        else:
            scratch.insert(0, acc)
        specs = [smem, *[vmem] * len(before), tuple(vmem for _ in total), *[vmem] * len(after)]
        return call(kernel, specs, outs, scratch, cost=apply_cost)(kept, *before, total, *after)

    def moved(value, target):
        return lax.ppermute(value, "sec", [(n, target(n) % sections) for n in range(sections)])

    def added(*values, after=()):
        kernel = functools.partial(add, len(values))
        specs = [vmem] * (len(values) + len(after))
        return call(kernel, specs, halves[:1], (), 2 * MIB, name="add")(*values, *after)[0]

    def between(chip):
        count = sections // 2
        return lambda n: 2 * (chip(n // 2, 1 if n // 2 % 2 else -1) % count) + n % 2

    cores = [[n, n + 1] for n in range(0, sections, 2)]
    near = [between(lambda z, up, far=far: z + up * far) for far in (2, 1, 3)]

    def summed(mine, theirs, after=(), beside=None, gathered=GATHERED):
        total = added(mine, moved(theirs, lambda n: n ^ 1))
        if beside is not None:
            beside(total)
        total = added(total, moved(total, lambda n: n ^ 2))
        parts = [moved(total, target) for target in near]
        total = added(total, *parts, after=after)
        if gathered:
            return (lax.all_gather(total, "sec", axis=0, axis_index_groups=cores),)
        return total, moved(total, lambda n: n ^ 1)

    blocks = shape(terms, states, states)
    left, right = left_env, right_env
    vector, mine, theirs, *applied = call(
        first_start, [smem, *[vmem] * 3], [block, *halves, block], cost=apply_cost
    )(kept, psi_one, left, right)

    slabs = terms // 2 + terms % 2 + 1
    sent = []

    def hand_over(ready):
        (package,) = call(
            pack,
            [smem, vmem, vmem, vmem],
            [shape(slabs * states + 16 * (terms // 2), states)],
            (),
        )(mpo_gain, left, edge_site, ready)
        sent.append(lax.ppermute(package, "seg", [(n, n + 1) for n in range(segments - 1)]))

    for step in range(ITERS - 1):
        total = summed(mine, theirs, beside=None if step else hand_over)
        vector, mine, theirs, *applied = step_call(
            first_step, (vector, *applied), total, (left, right), step
        )

    incoming, edge, second_vector, turned = call(
        unpack,
        [smem, smem, vmem, vmem, vmem],
        [blocks, shape(states, states), block, shape(states, states)],
        (),
    )(kept, mpo_gain, left, sent[0], psi_two)

    total = summed(mine, theirs, (turned,))
    first_rows, site, mine, theirs, *applied = call(
        second_start,
        [smem, vmem, tuple(vmem for _ in total), *[vmem] * 4],
        [rows, shape(states, states), *halves, block],
        cost=apply_cost,
    )(kept, vector, total, turned, edge, incoming, right)
    vector = second_vector
    for step in range(ITERS - 1):
        total = summed(mine, theirs)
        vector, mine, theirs, *applied = step_call(
            second_step, (vector, *applied), total, (site, edge, incoming, right), step
        )
    total = summed(mine, theirs, gathered=True)
    (second_rows,) = call(second_end, [smem, vmem, tuple(vmem for _ in total)], [rows])(
        kept, vector, total
    )
    return first_rows, second_rows


def solution(mesh):
    placed = (
        P("seg", "sec", None, None),
        P("seg", "sec", None, None),
        P("seg", None, None),
        P("seg", None, None),
        P("seg", None, None),
        P("seg", "sec"),
        P("seg", None),
    )
    return jax.shard_map(
        on_device,
        mesh=mesh,
        in_specs=placed,
        out_specs=(P("seg", "sec", None), P("seg", "sec", None)),
        check_vma=False,
    )
```

profile of v0, /device:TPU:1, one launch (start us, length us, event | category | flops | bytes accessed | tf_op | source)
XLA Modules:
  0.0 141.3 jit_solution(1038326133788961360)
XLA Ops:
  0.6 1.9 %copy-done = bf16[1,25,256,256]{3,2,1,0:T(8,128)(2,1)S(1)} copy-done((bf16[1,25,256,256]{3,2,1,0:T(8,128)(2,1)S(1)}, bf16[1,25,256,256]{3,2,1,0:T(8,128)(2,1)}, u32[]{:S(2)}) %copy-start) | copy-done | bytes 3276824
  2.6 1.9 %copy-done.2 = bf16[1,25,256,256]{3,2,1,0:T(8,128)(2,1)S(1)} copy-done((bf16[1,25,256,256]{3,2,1,0:T(8,128)(2,1)S(1)}, bf16[1,25,256,256]{3,2,1,0:T(8,128)(2,1)}, u32[]{:S(2)}) %copy-start.2) | copy-done | bytes 3276824
  6.1 2.7 %first_start.1 = (f32[256,256]{1,0:T(8,128)S(1)}, bf16[128,256]{1,0:T(8,128)(2,1)S(1)}, bf16[128,256]{1,0:T(8,128)(2,1)S(1)}, f32[256,256]{1,0:T(8,128)S(1)}) custom-call(s32[1,2]{1,0:T(1,128)S(1)} %copy-done.7, bf16[1,256,256]{2,1,0:T(8,128)(2,1)S(1)} %copy-done.4, bf16[1,25,256,256]{3,2,1,0:T(8,128)(2,1)S(1)} %copy-done.2, ...), custom_call_target="tpu_custom_call" | custom-call | flops 1677721600 | bytes 6553600 | tf_op jit(solution)/shard_map/first_start/pallas_call | solution.py:284
  8.7 3.3 %collective-permute-start = (bf16[128,256]{1,0:T(8,128)(2,1)S(1)}, bf16[128,256]{1,0:T(8,128)(2,1)S(1)}, u32[]{:S(2)}, u32[]{:S(2)}) collective-permute-start(bf16[128,256]{1,0:T(8,128)(2,1)S(1)} %get-tuple-element.32), channel_id=1, source_target_pairs={{0,1},{1,0},{2,3},{3,2},{4,5},{5,4},{6,7},{7,6},{8,9},{9,8},{10,11... | collective-permute-start | bytes 196616 | tf_op jit(solution)/shard_map/ppermute | solution.py:257
  19.2 6.4 %collective-permute-start.4 = (bf16[128,256]{1,0:T(8,128)(2,1)S(1)}, bf16[128,256]{1,0:T(8,128)(2,1)S(1)}, u32[]{:S(2)}, u32[]{:S(2)}) collective-permute-start(bf16[128,256]{1,0:T(8,128)(2,1)S(1)} %add.19.refs_0_), channel_id=1, source_target_pairs={{0,10},{1,11},{2,8},{3,9},{4,14},{5,15},{6,12},{7,13},{8,2},{9,3},... | collective-permute-start | bytes 196616 | tf_op jit(solution)/shard_map/ppermute | solution.py:257
  27.2 2.9 %collective-permute-done.3.refs_2_ = bf16[128,256]{1,0:T(8,128)(2,1)S(1)} collective-permute-done((bf16[128,256]{1,0:T(8,128)(2,1)S(1)}, bf16[128,256]{1,0:T(8,128)(2,1)S(1)}, u32[]{:S(2)}, u32[]{:S(2)}) %collective-permute-start.3) | collective-permute-done | bytes 65568 | tf_op jit(solution)/shard_map/ppermute | solution.py:257
  30.9 4.0 %all-gather = bf16[256,256]{1,0:T(8,128)(2,1)S(1)} all-gather(bf16[128,256]{1,0:T(8,128)(2,1)S(1)} %add.20), channel_id=2, replica_groups={{0,1},{2,3},{4,5},{6,7},{8,9},{10,11},{12,13},{14,15},{16,17},{18,19},{..., dimensions={0}, use_global_device_ids=true | all-gather | bytes 196608 | tf_op jit(solution)/shard_map/all_gather | solution.py:279
  34.9 2.7 %first_step.2 = (f32[256,256]{1,0:T(8,128)S(1)}, bf16[128,256]{1,0:T(8,128)(2,1)S(1)}, bf16[128,256]{1,0:T(8,128)(2,1)S(1)}, f32[256,256]{1,0:T(8,128)S(1)}) custom-call(s32[1,2]{1,0:T(1,128)S(1)} %copy-done.8, f32[256,256]{1,0:T(8,128)S(1)} %get-tuple-element.29.vector, f32[256,256]{1,0:T(8,128)S(1)} %get-tuple-element.30.applied, ...), custom_call_target="tpu_custom_call" | custom-call | flops 1677721600 | bytes 6553600 | tf_op jit(solution)/shard_map/first_step/pallas_call | solution.py:254
  39.0 2.5 %collective-permute-start.6 = (bf16[128,256]{1,0:T(8,128)(2,1)S(1)}, bf16[128,256]{1,0:T(8,128)(2,1)S(1)}, u32[]{:S(2)}, u32[]{:S(2)}) collective-permute-start(bf16[128,256]{1,0:T(8,128)(2,1)S(1)} %add.21.refs_0_), channel_id=1, source_target_pairs={{0,2},{1,3},{2,0},{3,1},{4,6},{5,7},{6,4},{7,5},{8,10},{9,11},{10,... | collective-permute-start | bytes 196616 | tf_op jit(solution)/shard_map/ppermute | solution.py:257
  41.5 2.2 %collective-permute-done.6.refs_1_ = bf16[128,256]{1,0:T(8,128)(2,1)S(1)} collective-permute-done((bf16[128,256]{1,0:T(8,128)(2,1)S(1)}, bf16[128,256]{1,0:T(8,128)(2,1)S(1)}, u32[]{:S(2)}, u32[]{:S(2)}) %collective-permute-start.6) | collective-permute-done | bytes 65568 | tf_op jit(solution)/shard_map/ppermute | solution.py:257
  43.7 2.1 %collective-permute-start.9 = (bf16[128,256]{1,0:T(8,128)(2,1)S(1)}, bf16[128,256]{1,0:T(8,128)(2,1)S(1)}, u32[]{:S(2)}, u32[]{:S(2)}) collective-permute-start(bf16[128,256]{1,0:T(8,128)(2,1)S(1)} %add.22.refs_0_), channel_id=1, source_target_pairs={{0,10},{1,11},{2,8},{3,9},{4,14},{5,15},{6,12},{7,13},{8,2},{9,3},... | collective-permute-start | bytes 196616 | tf_op jit(solution)/shard_map/ppermute | solution.py:257
  53.0 3.7 %all-gather.1 = bf16[256,256]{1,0:T(8,128)(2,1)S(1)} all-gather(bf16[128,256]{1,0:T(8,128)(2,1)S(1)} %add.23), channel_id=3, replica_groups={{0,1},{2,3},{4,5},{6,7},{8,9},{10,11},{12,13},{14,15},{16,17},{18,19},{..., dimensions={0}, use_global_device_ids=true | all-gather | bytes 196608 | tf_op jit(solution)/shard_map/all_gather | solution.py:279
  56.7 2.7 %first_step.3 = (f32[256,256]{1,0:T(8,128)S(1)}, bf16[128,256]{1,0:T(8,128)(2,1)S(1)}, bf16[128,256]{1,0:T(8,128)(2,1)S(1)}) custom-call(s32[1,2]{1,0:T(1,128)S(1)} %copy-done.8, f32[256,256]{1,0:T(8,128)S(1)} %get-tuple-element.33.vector, f32[256,256]{1,0:T(8,128)S(1)} %get-tuple-element.34.applied, bf16[2,128,256]{2,1,0:T(8,128)(2,1)S(1)} %bitcast.10, ...), custom_call_target="tpu_custom_call" | custom-call | flops 1677721600 | bytes 6553600 | tf_op jit(solution)/shard_map/first_step/pallas_call | solution.py:254
  61.9 2.0 %collective-permute-done.11.refs_1_ = bf16[128,256]{1,0:T(8,128)(2,1)S(1)} collective-permute-done((bf16[128,256]{1,0:T(8,128)(2,1)S(1)}, bf16[128,256]{1,0:T(8,128)(2,1)S(1)}, u32[]{:S(2)}, u32[]{:S(2)}) %collective-permute-start.11) | collective-permute-done | bytes 65568 | tf_op jit(solution)/shard_map/ppermute | solution.py:257
  64.0 2.6 %collective-permute-start.14 = (bf16[128,256]{1,0:T(8,128)(2,1)S(1)}, bf16[128,256]{1,0:T(8,128)(2,1)S(1)}, u32[]{:S(2)}, u32[]{:S(2)}) collective-permute-start(bf16[128,256]{1,0:T(8,128)(2,1)S(1)} %add.25.refs_0_), channel_id=1, source_target_pairs={{0,10},{1,11},{2,8},{3,9},{4,14},{5,15},{6,12},{7,13},{8,2},{9,3},... | collective-permute-start | bytes 196616 | tf_op jit(solution)/shard_map/ppermute | solution.py:257
  71.1 1.9 %collective-permute-done.12.refs_1_ = bf16[128,256]{1,0:T(8,128)(2,1)S(1)} collective-permute-done((bf16[128,256]{1,0:T(8,128)(2,1)S(1)}, bf16[128,256]{1,0:T(8,128)(2,1)S(1)}, u32[]{:S(2)}, u32[]{:S(2)}) %collective-permute-start.12) | collective-permute-done | bytes 65568 | tf_op jit(solution)/shard_map/ppermute | solution.py:257
  73.1 4.0 %all-gather.2 = bf16[256,256]{1,0:T(8,128)(2,1)S(1)} all-gather(bf16[128,256]{1,0:T(8,128)(2,1)S(1)} %add.26), channel_id=4, replica_groups={{0,1},{2,3},{4,5},{6,7},{8,9},{10,11},{12,13},{14,15},{16,17},{18,19},{..., dimensions={0}, use_global_device_ids=true | all-gather | bytes 196608 | tf_op jit(solution)/shard_map/all_gather | solution.py:279
  77.1 3.5 %second_start.1 = (f32[1,16,256]{2,1,0:T(8,128)}, bf16[256,256]{1,0:T(8,128)(2,1)S(1)}, bf16[128,256]{1,0:T(8,128)(2,1)S(1)}, bf16[128,256]{1,0:T(8,128)(2,1)S(1)}, f32[256,256]{1,0:T(8,128)S(1)}) custom-call(s32[1,2]{1,0:T(1,128)S(1)} %copy-done.8, f32[256,256]{1,0:T(8,128)S(1)} %get-tuple-element.37.vector, bf16[2,128,256]{2,1,0:T(8,128)(2,1)S(1)} %bitcast.7, ...), custom_call_target="tpu_custom_call" | custom-call | flops 1677721600 | bytes 6553600 | tf_op jit(solution)/shard_map/second_start/pallas_call | solution.py:314
  82.9 2.2 %collective-permute-done.17.refs_1_ = bf16[128,256]{1,0:T(8,128)(2,1)S(1)} collective-permute-done((bf16[128,256]{1,0:T(8,128)(2,1)S(1)}, bf16[128,256]{1,0:T(8,128)(2,1)S(1)}, u32[]{:S(2)}, u32[]{:S(2)}) %collective-permute-start.17) | collective-permute-done | bytes 65568 | tf_op jit(solution)/shard_map/ppermute | solution.py:257
  85.2 2.4 %collective-permute-start.20 = (bf16[128,256]{1,0:T(8,128)(2,1)S(1)}, bf16[128,256]{1,0:T(8,128)(2,1)S(1)}, u32[]{:S(2)}, u32[]{:S(2)}) collective-permute-start(bf16[128,256]{1,0:T(8,128)(2,1)S(1)} %add.28.refs_0_), channel_id=1, source_target_pairs={{0,10},{1,11},{2,8},{3,9},{4,14},{5,15},{6,12},{7,13},{8,2},{9,3},... | collective-permute-start | bytes 196616 | tf_op jit(solution)/shard_map/ppermute | solution.py:257
  92.3 2.2 %collective-permute-done.18.refs_1_ = bf16[128,256]{1,0:T(8,128)(2,1)S(1)} collective-permute-done((bf16[128,256]{1,0:T(8,128)(2,1)S(1)}, bf16[128,256]{1,0:T(8,128)(2,1)S(1)}, u32[]{:S(2)}, u32[]{:S(2)}) %collective-permute-start.18) | collective-permute-done | bytes 65568 | tf_op jit(solution)/shard_map/ppermute | solution.py:257
  94.5 3.4 %all-gather.3 = bf16[256,256]{1,0:T(8,128)(2,1)S(1)} all-gather(bf16[128,256]{1,0:T(8,128)(2,1)S(1)} %add.29), channel_id=5, replica_groups={{0,1},{2,3},{4,5},{6,7},{8,9},{10,11},{12,13},{14,15},{16,17},{18,19},{..., dimensions={0}, use_global_device_ids=true | all-gather | bytes 196608 | tf_op jit(solution)/shard_map/all_gather | solution.py:279
  97.9 3.4 %second_step.2 = (f32[256,256]{1,0:T(8,128)S(1)}, bf16[128,256]{1,0:T(8,128)(2,1)S(1)}, bf16[128,256]{1,0:T(8,128)(2,1)S(1)}, f32[256,256]{1,0:T(8,128)S(1)}) custom-call(s32[1,2]{1,0:T(1,128)S(1)} %copy-done.8, f32[256,256]{1,0:T(8,128)S(1)} %get-tuple-element.44.vector, f32[256,256]{1,0:T(8,128)S(1)} %get-tuple-element.45.applied, ...), custom_call_target="tpu_custom_call" | custom-call | flops 1677721600 | bytes 6553600 | tf_op jit(solution)/shard_map/second_step/pallas_call | solution.py:254
  103.9 2.0 %collective-permute-done.22.refs_1_ = bf16[128,256]{1,0:T(8,128)(2,1)S(1)} collective-permute-done((bf16[128,256]{1,0:T(8,128)(2,1)S(1)}, bf16[128,256]{1,0:T(8,128)(2,1)S(1)}, u32[]{:S(2)}, u32[]{:S(2)}) %collective-permute-start.22) | collective-permute-done | bytes 65568 | tf_op jit(solution)/shard_map/ppermute | solution.py:257
  105.9 2.7 %collective-permute-start.25 = (bf16[128,256]{1,0:T(8,128)(2,1)S(1)}, bf16[128,256]{1,0:T(8,128)(2,1)S(1)}, u32[]{:S(2)}, u32[]{:S(2)}) collective-permute-start(bf16[128,256]{1,0:T(8,128)(2,1)S(1)} %add.31.refs_0_), channel_id=1, source_target_pairs={{0,10},{1,11},{2,8},{3,9},{4,14},{5,15},{6,12},{7,13},{8,2},{9,3},... | collective-permute-start | bytes 196616 | tf_op jit(solution)/shard_map/ppermute | solution.py:257
  113.1 2.5 %collective-permute-done.23.refs_1_ = bf16[128,256]{1,0:T(8,128)(2,1)S(1)} collective-permute-done((bf16[128,256]{1,0:T(8,128)(2,1)S(1)}, bf16[128,256]{1,0:T(8,128)(2,1)S(1)}, u32[]{:S(2)}, u32[]{:S(2)}) %collective-permute-start.23) | collective-permute-done | bytes 65568 | tf_op jit(solution)/shard_map/ppermute | solution.py:257
  115.6 3.4 %all-gather.4 = bf16[256,256]{1,0:T(8,128)(2,1)S(1)} all-gather(bf16[128,256]{1,0:T(8,128)(2,1)S(1)} %add.32), channel_id=6, replica_groups={{0,1},{2,3},{4,5},{6,7},{8,9},{10,11},{12,13},{14,15},{16,17},{18,19},{..., dimensions={0}, use_global_device_ids=true | all-gather | bytes 196608 | tf_op jit(solution)/shard_map/all_gather | solution.py:279
  119.0 3.4 %second_step.3 = (f32[256,256]{1,0:T(8,128)S(1)}, bf16[128,256]{1,0:T(8,128)(2,1)S(1)}, bf16[128,256]{1,0:T(8,128)(2,1)S(1)}) custom-call(s32[1,2]{1,0:T(1,128)S(1)} %copy-done.8, f32[256,256]{1,0:T(8,128)S(1)} %get-tuple-element.49.vector, f32[256,256]{1,0:T(8,128)S(1)} %get-tuple-element.50.applied, bf16[2,128,256]{2,1,0:T(8,128)(2,1)S(1)} %bitcast.6, ...), custom_call_target="tpu_custom_call" | custom-call | flops 1677721600 | bytes 6553600 | tf_op jit(solution)/shard_map/second_step/pallas_call | solution.py:254
  124.8 2.2 %collective-permute-done.27.refs_1_ = bf16[128,256]{1,0:T(8,128)(2,1)S(1)} collective-permute-done((bf16[128,256]{1,0:T(8,128)(2,1)S(1)}, bf16[128,256]{1,0:T(8,128)(2,1)S(1)}, u32[]{:S(2)}, u32[]{:S(2)}) %collective-permute-start.27) | collective-permute-done | bytes 65568 | tf_op jit(solution)/shard_map/ppermute | solution.py:257
  126.9 2.5 %collective-permute-start.30 = (bf16[128,256]{1,0:T(8,128)(2,1)S(1)}, bf16[128,256]{1,0:T(8,128)(2,1)S(1)}, u32[]{:S(2)}, u32[]{:S(2)}) collective-permute-start(bf16[128,256]{1,0:T(8,128)(2,1)S(1)} %add.34.refs_0_), channel_id=1, source_target_pairs={{0,10},{1,11},{2,8},{3,9},{4,14},{5,15},{6,12},{7,13},{8,2},{9,3},... | collective-permute-start | bytes 196616 | tf_op jit(solution)/shard_map/ppermute | solution.py:257
  134.1 2.2 %collective-permute-done.28.refs_1_ = bf16[128,256]{1,0:T(8,128)(2,1)S(1)} collective-permute-done((bf16[128,256]{1,0:T(8,128)(2,1)S(1)}, bf16[128,256]{1,0:T(8,128)(2,1)S(1)}, u32[]{:S(2)}, u32[]{:S(2)}) %collective-permute-start.28) | collective-permute-done | bytes 65568 | tf_op jit(solution)/shard_map/ppermute | solution.py:257
  136.4 3.4 %all-gather.5 = bf16[256,256]{1,0:T(8,128)(2,1)S(1)} all-gather(bf16[128,256]{1,0:T(8,128)(2,1)S(1)} %add.35), channel_id=7, replica_groups={{0,1},{2,3},{4,5},{6,7},{8,9},{10,11},{12,13},{14,15},{16,17},{18,19},{..., dimensions={0}, use_global_device_ids=true | all-gather | bytes 196608 | tf_op jit(solution)/shard_map/all_gather | solution.py:279
  (83 shorter events, 49.7 us)
Async XLA Ops:
  8.7 26.2 %copy-start.1 = (bf16[1,25,256,256]{3,2,1,0:T(8,128)(2,1)S(1)}, bf16[1,25,256,256]{3,2,1,0:T(8,128)(2,1)}, u32[]{:S(2)}) copy-start(bf16[1,25,256,256]{3,2,1,0:T(8,128)(2,1)} %right.11) | copy-start | bytes 9830404
  8.7 4.2 %collective-permute-start = (bf16[128,256]{1,0:T(8,128)(2,1)S(1)}, bf16[128,256]{1,0:T(8,128)(2,1)S(1)}, u32[]{:S(2)}, u32[]{:S(2)}) collective-permute-start(bf16[128,256]{1,0:T(8,128)(2,1)S(1)} %get-tuple-element.32), channel_id=1, source_target_pairs={{0,1},{1,0},{2,3},{3,2},{4,5},{5,4},{6,7},{7,6},{8,9},{9,8},{10,11... | collective-permute-start | bytes 196616 | tf_op jit(solution)/shard_map/ppermute | solution.py:257
  14.2 54.6 %collective-permute-start.15 = (bf16[3776,256]{1,0:T(8,128)(2,1)S(1)}, bf16[3776,256]{1,0:T(8,128)(2,1)S(1)}, u32[]{:S(2)}, u32[]{:S(2)}) collective-permute-start(bf16[3776,256]{1,0:T(8,128)(2,1)S(1)} %pack.1), channel_id=1, source_target_pairs={{0,16},{16,32},{32,48},{48,64},{64,80},{80,96},{96,112},{112,128},... | collective-permute-start | bytes 5799944 | tf_op jit(solution)/shard_map/ppermute | solution.py:298
  15.8 3.4 %collective-permute-start.1 = (bf16[128,256]{1,0:T(8,128)(2,1)S(1)}, bf16[128,256]{1,0:T(8,128)(2,1)S(1)}, u32[]{:S(2)}, u32[]{:S(2)}) collective-permute-start(bf16[128,256]{1,0:T(8,128)(2,1)S(1)} %add.18.refs_0_.ready), channel_id=1, source_target_pairs={{0,2},{1,3},{2,0},{3,1},{4,6},{5,7},{6,4},{7,5},{8,10},{9,11},{10,... | collective-permute-start | bytes 196616 | tf_op jit(solution)/shard_map/ppermute | solution.py:257
  19.2 8.0 %collective-permute-start.4 = (bf16[128,256]{1,0:T(8,128)(2,1)S(1)}, bf16[128,256]{1,0:T(8,128)(2,1)S(1)}, u32[]{:S(2)}, u32[]{:S(2)}) collective-permute-start(bf16[128,256]{1,0:T(8,128)(2,1)S(1)} %add.19.refs_0_), channel_id=1, source_target_pairs={{0,10},{1,11},{2,8},{3,9},{4,14},{5,15},{6,12},{7,13},{8,2},{9,3},... | collective-permute-start | bytes 196616 | tf_op jit(solution)/shard_map/ppermute | solution.py:257
  25.5 4.5 %collective-permute-start.3 = (bf16[128,256]{1,0:T(8,128)(2,1)S(1)}, bf16[128,256]{1,0:T(8,128)(2,1)S(1)}, u32[]{:S(2)}, u32[]{:S(2)}) collective-permute-start(bf16[128,256]{1,0:T(8,128)(2,1)S(1)} %add.19.refs_0_), channel_id=1, source_target_pairs={{0,14},{1,15},{2,4},{3,5},{4,2},{5,3},{6,8},{7,9},{8,6},{9,7},{10,... | collective-permute-start | bytes 196616 | tf_op jit(solution)/shard_map/ppermute | solution.py:257
  25.5 5.3 %collective-permute-start.2 = (bf16[128,256]{1,0:T(8,128)(2,1)S(1)}, bf16[128,256]{1,0:T(8,128)(2,1)S(1)}, u32[]{:S(2)}, u32[]{:S(2)}) collective-permute-start(bf16[128,256]{1,0:T(8,128)(2,1)S(1)} %add.19.refs_0_), channel_id=1, source_target_pairs={{0,12},{1,13},{2,6},{3,7},{4,0},{5,1},{6,10},{7,11},{8,4},{9,5},{1... | collective-permute-start | bytes 196616 | tf_op jit(solution)/shard_map/ppermute | solution.py:257
  37.6 1.3 collective-permute-start.5
  39.0 4.7 %collective-permute-start.6 = (bf16[128,256]{1,0:T(8,128)(2,1)S(1)}, bf16[128,256]{1,0:T(8,128)(2,1)S(1)}, u32[]{:S(2)}, u32[]{:S(2)}) collective-permute-start(bf16[128,256]{1,0:T(8,128)(2,1)S(1)} %add.21.refs_0_), channel_id=1, source_target_pairs={{0,2},{1,3},{2,0},{3,1},{4,6},{5,7},{6,4},{7,5},{8,10},{9,11},{10,... | collective-permute-start | bytes 196616 | tf_op jit(solution)/shard_map/ppermute | solution.py:257
  43.7 6.3 %collective-permute-start.9 = (bf16[128,256]{1,0:T(8,128)(2,1)S(1)}, bf16[128,256]{1,0:T(8,128)(2,1)S(1)}, u32[]{:S(2)}, u32[]{:S(2)}) collective-permute-start(bf16[128,256]{1,0:T(8,128)(2,1)S(1)} %add.22.refs_0_), channel_id=1, source_target_pairs={{0,10},{1,11},{2,8},{3,9},{4,14},{5,15},{6,12},{7,13},{8,2},{9,3},... | collective-permute-start | bytes 196616 | tf_op jit(solution)/shard_map/ppermute | solution.py:257
  45.8 5.3 %collective-permute-start.8 = (bf16[128,256]{1,0:T(8,128)(2,1)S(1)}, bf16[128,256]{1,0:T(8,128)(2,1)S(1)}, u32[]{:S(2)}, u32[]{:S(2)}) collective-permute-start(bf16[128,256]{1,0:T(8,128)(2,1)S(1)} %add.22.refs_0_), channel_id=1, source_target_pairs={{0,14},{1,15},{2,4},{3,5},{4,2},{5,3},{6,8},{7,9},{8,6},{9,7},{10,... | collective-permute-start | bytes 196616 | tf_op jit(solution)/shard_map/ppermute | solution.py:257
  47.5 5.4 %collective-permute-start.7 = (bf16[128,256]{1,0:T(8,128)(2,1)S(1)}, bf16[128,256]{1,0:T(8,128)(2,1)S(1)}, u32[]{:S(2)}, u32[]{:S(2)}) collective-permute-start(bf16[128,256]{1,0:T(8,128)(2,1)S(1)} %add.22.refs_0_), channel_id=1, source_target_pairs={{0,12},{1,13},{2,6},{3,7},{4,0},{5,1},{6,10},{7,11},{8,4},{9,5},{1... | collective-permute-start | bytes 196616 | tf_op jit(solution)/shard_map/ppermute | solution.py:257
  59.4 1.3 collective-permute-start.10
  60.7 3.2 %collective-permute-start.11 = (bf16[128,256]{1,0:T(8,128)(2,1)S(1)}, bf16[128,256]{1,0:T(8,128)(2,1)S(1)}, u32[]{:S(2)}, u32[]{:S(2)}) collective-permute-start(bf16[128,256]{1,0:T(8,128)(2,1)S(1)} %add.24.refs_0_), channel_id=1, source_target_pairs={{0,2},{1,3},{2,0},{3,1},{4,6},{5,7},{6,4},{7,5},{8,10},{9,11},{10,... | collective-permute-start | bytes 196616 | tf_op jit(solution)/shard_map/ppermute | solution.py:257
  64.0 6.4 %collective-permute-start.14 = (bf16[128,256]{1,0:T(8,128)(2,1)S(1)}, bf16[128,256]{1,0:T(8,128)(2,1)S(1)}, u32[]{:S(2)}, u32[]{:S(2)}) collective-permute-start(bf16[128,256]{1,0:T(8,128)(2,1)S(1)} %add.25.refs_0_), channel_id=1, source_target_pairs={{0,10},{1,11},{2,8},{3,9},{4,14},{5,15},{6,12},{7,13},{8,2},{9,3},... | collective-permute-start | bytes 196616 | tf_op jit(solution)/shard_map/ppermute | solution.py:257
  66.6 4.5 %collective-permute-start.13 = (bf16[128,256]{1,0:T(8,128)(2,1)S(1)}, bf16[128,256]{1,0:T(8,128)(2,1)S(1)}, u32[]{:S(2)}, u32[]{:S(2)}) collective-permute-start(bf16[128,256]{1,0:T(8,128)(2,1)S(1)} %add.25.refs_0_), channel_id=1, source_target_pairs={{0,14},{1,15},{2,4},{3,5},{4,2},{5,3},{6,8},{7,9},{8,6},{9,7},{10,... | collective-permute-start | bytes 196616 | tf_op jit(solution)/shard_map/ppermute | solution.py:257
  68.0 5.1 %collective-permute-start.12 = (bf16[128,256]{1,0:T(8,128)(2,1)S(1)}, bf16[128,256]{1,0:T(8,128)(2,1)S(1)}, u32[]{:S(2)}, u32[]{:S(2)}) collective-permute-start(bf16[128,256]{1,0:T(8,128)(2,1)S(1)} %add.25.refs_0_), channel_id=1, source_target_pairs={{0,12},{1,13},{2,6},{3,7},{4,0},{5,1},{6,10},{7,11},{8,4},{9,5},{1... | collective-permute-start | bytes 196616 | tf_op jit(solution)/shard_map/ppermute | solution.py:257
  80.6 1.3 collective-permute-start.16
  82.0 3.2 %collective-permute-start.17 = (bf16[128,256]{1,0:T(8,128)(2,1)S(1)}, bf16[128,256]{1,0:T(8,128)(2,1)S(1)}, u32[]{:S(2)}, u32[]{:S(2)}) collective-permute-start(bf16[128,256]{1,0:T(8,128)(2,1)S(1)} %add.27.refs_0_), channel_id=1, source_target_pairs={{0,2},{1,3},{2,0},{3,1},{4,6},{5,7},{6,4},{7,5},{8,10},{9,11},{10,... | collective-permute-start | bytes 196616 | tf_op jit(solution)/shard_map/ppermute | solution.py:257
  85.2 6.2 %collective-permute-start.20 = (bf16[128,256]{1,0:T(8,128)(2,1)S(1)}, bf16[128,256]{1,0:T(8,128)(2,1)S(1)}, u32[]{:S(2)}, u32[]{:S(2)}) collective-permute-start(bf16[128,256]{1,0:T(8,128)(2,1)S(1)} %add.28.refs_0_), channel_id=1, source_target_pairs={{0,10},{1,11},{2,8},{3,9},{4,14},{5,15},{6,12},{7,13},{8,2},{9,3},... | collective-permute-start | bytes 196616 | tf_op jit(solution)/shard_map/ppermute | solution.py:257
  87.6 4.7 %collective-permute-start.19 = (bf16[128,256]{1,0:T(8,128)(2,1)S(1)}, bf16[128,256]{1,0:T(8,128)(2,1)S(1)}, u32[]{:S(2)}, u32[]{:S(2)}) collective-permute-start(bf16[128,256]{1,0:T(8,128)(2,1)S(1)} %add.28.refs_0_), channel_id=1, source_target_pairs={{0,14},{1,15},{2,4},{3,5},{4,2},{5,3},{6,8},{7,9},{8,6},{9,7},{10,... | collective-permute-start | bytes 196616 | tf_op jit(solution)/shard_map/ppermute | solution.py:257
  89.0 5.5 %collective-permute-start.18 = (bf16[128,256]{1,0:T(8,128)(2,1)S(1)}, bf16[128,256]{1,0:T(8,128)(2,1)S(1)}, u32[]{:S(2)}, u32[]{:S(2)}) collective-permute-start(bf16[128,256]{1,0:T(8,128)(2,1)S(1)} %add.28.refs_0_), channel_id=1, source_target_pairs={{0,12},{1,13},{2,6},{3,7},{4,0},{5,1},{6,10},{7,11},{8,4},{9,5},{1... | collective-permute-start | bytes 196616 | tf_op jit(solution)/shard_map/ppermute | solution.py:257
  101.3 1.3 collective-permute-start.21
  102.6 3.2 %collective-permute-start.22 = (bf16[128,256]{1,0:T(8,128)(2,1)S(1)}, bf16[128,256]{1,0:T(8,128)(2,1)S(1)}, u32[]{:S(2)}, u32[]{:S(2)}) collective-permute-start(bf16[128,256]{1,0:T(8,128)(2,1)S(1)} %add.30.refs_0_), channel_id=1, source_target_pairs={{0,2},{1,3},{2,0},{3,1},{4,6},{5,7},{6,4},{7,5},{8,10},{9,11},{10,... | collective-permute-start | bytes 196616 | tf_op jit(solution)/shard_map/ppermute | solution.py:257
  105.9 6.3 %collective-permute-start.25 = (bf16[128,256]{1,0:T(8,128)(2,1)S(1)}, bf16[128,256]{1,0:T(8,128)(2,1)S(1)}, u32[]{:S(2)}, u32[]{:S(2)}) collective-permute-start(bf16[128,256]{1,0:T(8,128)(2,1)S(1)} %add.31.refs_0_), channel_id=1, source_target_pairs={{0,10},{1,11},{2,8},{3,9},{4,14},{5,15},{6,12},{7,13},{8,2},{9,3},... | collective-permute-start | bytes 196616 | tf_op jit(solution)/shard_map/ppermute | solution.py:257
  108.5 4.5 %collective-permute-start.24 = (bf16[128,256]{1,0:T(8,128)(2,1)S(1)}, bf16[128,256]{1,0:T(8,128)(2,1)S(1)}, u32[]{:S(2)}, u32[]{:S(2)}) collective-permute-start(bf16[128,256]{1,0:T(8,128)(2,1)S(1)} %add.31.refs_0_), channel_id=1, source_target_pairs={{0,14},{1,15},{2,4},{3,5},{4,2},{5,3},{6,8},{7,9},{8,6},{9,7},{10,... | collective-permute-start | bytes 196616 | tf_op jit(solution)/shard_map/ppermute | solution.py:257
  109.9 5.6 %collective-permute-start.23 = (bf16[128,256]{1,0:T(8,128)(2,1)S(1)}, bf16[128,256]{1,0:T(8,128)(2,1)S(1)}, u32[]{:S(2)}, u32[]{:S(2)}) collective-permute-start(bf16[128,256]{1,0:T(8,128)(2,1)S(1)} %add.31.refs_0_), channel_id=1, source_target_pairs={{0,12},{1,13},{2,6},{3,7},{4,0},{5,1},{6,10},{7,11},{8,4},{9,5},{1... | collective-permute-start | bytes 196616 | tf_op jit(solution)/shard_map/ppermute | solution.py:257
  122.4 1.3 collective-permute-start.26
  123.7 3.2 %collective-permute-start.27 = (bf16[128,256]{1,0:T(8,128)(2,1)S(1)}, bf16[128,256]{1,0:T(8,128)(2,1)S(1)}, u32[]{:S(2)}, u32[]{:S(2)}) collective-permute-start(bf16[128,256]{1,0:T(8,128)(2,1)S(1)} %add.33.refs_0_), channel_id=1, source_target_pairs={{0,2},{1,3},{2,0},{3,1},{4,6},{5,7},{6,4},{7,5},{8,10},{9,11},{10,... | collective-permute-start | bytes 196616 | tf_op jit(solution)/shard_map/ppermute | solution.py:257
  126.9 6.3 %collective-permute-start.30 = (bf16[128,256]{1,0:T(8,128)(2,1)S(1)}, bf16[128,256]{1,0:T(8,128)(2,1)S(1)}, u32[]{:S(2)}, u32[]{:S(2)}) collective-permute-start(bf16[128,256]{1,0:T(8,128)(2,1)S(1)} %add.34.refs_0_), channel_id=1, source_target_pairs={{0,10},{1,11},{2,8},{3,9},{4,14},{5,15},{6,12},{7,13},{8,2},{9,3},... | collective-permute-start | bytes 196616 | tf_op jit(solution)/shard_map/ppermute | solution.py:257
  129.4 4.6 %collective-permute-start.29 = (bf16[128,256]{1,0:T(8,128)(2,1)S(1)}, bf16[128,256]{1,0:T(8,128)(2,1)S(1)}, u32[]{:S(2)}, u32[]{:S(2)}) collective-permute-start(bf16[128,256]{1,0:T(8,128)(2,1)S(1)} %add.34.refs_0_), channel_id=1, source_target_pairs={{0,14},{1,15},{2,4},{3,5},{4,2},{5,3},{6,8},{7,9},{8,6},{9,7},{10,... | collective-permute-start | bytes 196616 | tf_op jit(solution)/shard_map/ppermute | solution.py:257
  130.8 5.5 %collective-permute-start.28 = (bf16[128,256]{1,0:T(8,128)(2,1)S(1)}, bf16[128,256]{1,0:T(8,128)(2,1)S(1)}, u32[]{:S(2)}, u32[]{:S(2)}) collective-permute-start(bf16[128,256]{1,0:T(8,128)(2,1)S(1)} %add.34.refs_0_), channel_id=1, source_target_pairs={{0,12},{1,13},{2,6},{3,7},{4,0},{5,1},{6,10},{7,11},{8,4},{9,5},{1... | collective-permute-start | bytes 196616 | tf_op jit(solution)/shard_map/ppermute | solution.py:257
  (9 other events, 64.6 us)
where the time goes:
time: 142 us; the launch traced here: 141 us
  starting transfers between devices  46.7 us (33%)
  waiting for transfers between devices  43.5 us (31%)
  Pallas kernels  23.1 us (16%)
  blocking collectives  21.8 us (15%)
  local copies, waits for them, and re-layouts  5.43 us (4%)
    ppermute x30, starting transfers between devices, moved(): lax.ppermute(value, 'sec', [(n, target(n) % sections) for n in range(sect...  45.2 us
    ppermute x30, waiting for transfers between devices, moved(): lax.ppermute(value, 'sec', [(n, target(n) % sections) for n in range(sect...  43.5 us
    all_gather x6, blocking collectives, summed(): return (lax.all_gather(total, 'sec', axis=0, axis_index_groups=cores),)  21.8 us
    pallas_call x4, Pallas kernels, step_call(): call(kernel, specs, outs, scratch, cost=apply_cost)  12.1 us
    unnamed x20, local copies, waits for them, and re-layouts  5.43 us
    pallas_call x1, Pallas kernels, on_device(): call(second_start, [smem, vmem, tuple((vmem for _ in total)), *[vmem] * 4...  3.52 us
  transfers between devices with their start and end apart: 31, of which 29 were waited for; matrix products, arithmetic and copies ran while one was open for 0% of the time, Pallas kernels for 5%

commit v1 on v0

--- a/solution.py
+++ b/solution.py
@@ -113,7 +113,7 @@
     return lax.broadcasted_iota(jnp.int32, shape, 0), lax.broadcasted_iota(jnp.int32, shape, 1)
 
 
-def pack(gain, left, edge, ready, package):
+def pack(gain, left, edge, package):
     terms, states = left.shape[1], left.shape[2]
     row, column = place((states, states))
     pairs = terms // 2
@@ -201,9 +201,14 @@
     hand_out(applied_after, mine, theirs)
 
 
-def second_end(kept, vector, summed, rows, acc):
-    acc[...] = stepped(vector, summed, kept[0, 1])
-    own_rows(acc, rows)
+def second_end(kept, vector, summed, rows):
+    live, share, half = kept[0, 1], rows.shape[1], summed[0].shape[1]
+    a, b = coefficients(vector[...], joined(summed, live))
+    start = lax.axis_index("sec") * share
+    part = pl.ds(pl.multiple_of(lax.rem(start, half), share), share)
+    product = summed[0][lax.div(start, half), part, :].astype(F32)
+    product = jnp.where(live_rows(product.shape, live - start), product, 0.0)
+    rows[0] = a * vector[pl.ds(pl.multiple_of(start, share), share), :] + b * product
 
 
 def add(count, *refs):
@@ -268,10 +273,8 @@
     cores = [[n, n + 1] for n in range(0, sections, 2)]
     near = [between(lambda z, up, far=far: z + up * far) for far in (2, 1, 3)]
 
-    def summed(mine, theirs, after=(), beside=None, gathered=GATHERED):
+    def summed(mine, theirs, after=(), gathered=GATHERED):
         total = added(mine, moved(theirs, lambda n: n ^ 1))
-        if beside is not None:
-            beside(total)
         total = added(total, moved(total, lambda n: n ^ 2))
         parts = [moved(total, target) for target in near]
         total = added(total, *parts, after=after)
@@ -281,24 +284,24 @@
 
     blocks = shape(terms, states, states)
     left, right = left_env, right_env
+    slabs = terms // 2 + terms % 2 + 1
+    (package,) = call(
+        pack,
+        [smem, vmem, vmem],
+        [shape(slabs * states + 16 * (terms // 2), states)],
+        (),
+        cost=pl.CostEstimate(
+            flops=60 * terms * states**3, bytes_accessed=4 * terms * states**2, transcendentals=0
+        ),
+    )(mpo_gain, left_env, edge_site)
+    package = lax.ppermute(package, "seg", [(n, n + 1) for n in range(segments - 1)])
+
     vector, mine, theirs, *applied = call(
         first_start, [smem, *[vmem] * 3], [block, *halves, block], cost=apply_cost
     )(kept, psi_one, left, right)
 
-    slabs = terms // 2 + terms % 2 + 1
-    sent = []
-
-    def hand_over(ready):
-        (package,) = call(
-            pack,
-            [smem, vmem, vmem, vmem],
-            [shape(slabs * states + 16 * (terms // 2), states)],
-            (),
-        )(mpo_gain, left, edge_site, ready)
-        sent.append(lax.ppermute(package, "seg", [(n, n + 1) for n in range(segments - 1)]))
-
     for step in range(ITERS - 1):
-        total = summed(mine, theirs, beside=None if step else hand_over)
+        total = summed(mine, theirs)
         vector, mine, theirs, *applied = step_call(
             first_step, (vector, *applied), total, (left, right), step
         )
@@ -308,7 +311,7 @@
         [smem, smem, vmem, vmem, vmem],
         [blocks, shape(states, states), block, shape(states, states)],
         (),
-    )(kept, mpo_gain, left, sent[0], psi_two)
+    )(kept, mpo_gain, left, package, psi_two)
 
     total = summed(mine, theirs, (turned,))
     first_rows, site, mine, theirs, *applied = call(
@@ -324,7 +327,7 @@
             second_step, (vector, *applied), total, (site, edge, incoming, right), step
         )
     total = summed(mine, theirs, gathered=True)
-    (second_rows,) = call(second_end, [smem, vmem, tuple(vmem for _ in total)], [rows])(
+    (second_rows,) = call(second_end, [smem, vmem, tuple(vmem for _ in total)], [rows], ())(
         kept, vector, total
     )
     return first_rows, second_rows

time: 142 us -> 140 us (0.986)
  local copies, waits for them, and re-layouts: 5.43 us -> 3.65 us
    ppermute x30, starting transfers between devices: 45.2 us -> 42.3 us  [moved(): lax.ppermute(value, 'sec', [(n, target(n) % sections) for n in range(sect...]
    ppermute x1, starting transfers between devices: 1.5 us -> 4.07 us  [on_device(): lax.ppermute(package, 'seg', [(n, n + 1) for n in range(segments - 1)])]
    unnamed x20 -> x18, local copies, waits for them, and re-layouts: 5.43 us -> 3.65 us
  transfers between devices with their start and end apart: 31 -> 31, of which waited for: 29 -> 29; matrix products, arithmetic and copies ran while one was open for 0% -> 0% of each run, Pallas kernels for 5% -> 7%
where the time goes in v1:
time: 140 us; the launch traced here: 139 us
  starting transfers between devices  46.4 us (33%)
  waiting for transfers between devices  43.8 us (31%)
  Pallas kernels  23 us (16%)
  blocking collectives  21.8 us (16%)
  local copies, waits for them, and re-layouts  3.65 us (3%)
    ppermute x30, waiting for transfers between devices, moved(): lax.ppermute(value, 'sec', [(n, target(n) % sections) for n in range(sect...  43.8 us
    ppermute x30, starting transfers between devices, moved(): lax.ppermute(value, 'sec', [(n, target(n) % sections) for n in range(sect...  42.3 us
    all_gather x6, blocking collectives, summed(): return (lax.all_gather(total, 'sec', axis=0, axis_index_groups=cores),)  21.8 us
    pallas_call x4, Pallas kernels, step_call(): call(kernel, specs, outs, scratch, cost=apply_cost)  12.1 us
    ppermute x1, starting transfers between devices, on_device(): lax.ppermute(package, 'seg', [(n, n + 1) for n in range(segments - 1)])  4.07 us
    unnamed x18, local copies, waits for them, and re-layouts  3.65 us
    pallas_call x1, Pallas kernels, on_device(): call(second_start, [smem, vmem, tuple((vmem for _ in total)), *[vmem] * 4...  3.52 us
  transfers between devices with their start and end apart: 31, of which 29 were waited for; matrix products, arithmetic and copies ran while one was open for 0% of the time, Pallas kernels for 7%

profile of v1, /device:TPU:1, one launch (start us, length us, event | category | flops | bytes accessed | tf_op | source)
XLA Modules:
  0.0 139.4 jit_solution(11540544772276774745)
XLA Ops:
  0.7 2.1 %copy-done.1 = bf16[1,25,256,256]{3,2,1,0:T(8,128)(2,1)S(1)} copy-done((bf16[1,25,256,256]{3,2,1,0:T(8,128)(2,1)S(1)}, bf16[1,25,256,256]{3,2,1,0:T(8,128)(2,1)}, u32[]{:S(2)}) %copy-start.1) | copy-done | bytes 3276824
  5.5 4.1 %collective-permute-start.15 = (bf16[3776,256]{1,0:T(8,128)(2,1)S(1)}, bf16[3776,256]{1,0:T(8,128)(2,1)S(1)}, u32[]{:S(2)}, u32[]{:S(2)}) collective-permute-start(bf16[3776,256]{1,0:T(8,128)(2,1)S(1)} %pack.1), channel_id=1, source_target_pairs={{0,16},{16,32},{32,48},{48,64},{64,80},{80,96},{96,112},{112,128},... | collective-permute-start | bytes 5799944 | tf_op jit(solution)/shard_map/ppermute | solution.py:297
  9.6 2.7 %first_start.1 = (f32[256,256]{1,0:T(8,128)S(1)}, bf16[128,256]{1,0:T(8,128)(2,1)S(1)}, bf16[128,256]{1,0:T(8,128)(2,1)S(1)}, f32[256,256]{1,0:T(8,128)S(1)}) custom-call(s32[1,2]{1,0:T(1,128)S(1)} %copy-done.5, bf16[1,256,256]{2,1,0:T(8,128)(2,1)S(1)} %copy-done.3, bf16[1,25,256,256]{3,2,1,0:T(8,128)(2,1)S(1)} %copy-done.2, ...), custom_call_target="tpu_custom_call" | custom-call | flops 1677721600 | bytes 6553600 | tf_op jit(solution)/shard_map/first_start/pallas_call | solution.py:299
  16.0 2.1 %collective-permute-done.1.refs_1_ = bf16[128,256]{1,0:T(8,128)(2,1)S(1)} collective-permute-done((bf16[128,256]{1,0:T(8,128)(2,1)S(1)}, bf16[128,256]{1,0:T(8,128)(2,1)S(1)}, u32[]{:S(2)}, u32[]{:S(2)}) %collective-permute-start.1) | collective-permute-done | bytes 65568 | tf_op jit(solution)/shard_map/ppermute | solution.py:262
  18.1 6.0 %collective-permute-start.4 = (bf16[128,256]{1,0:T(8,128)(2,1)S(1)}, bf16[128,256]{1,0:T(8,128)(2,1)S(1)}, u32[]{:S(2)}, u32[]{:S(2)}) collective-permute-start(bf16[128,256]{1,0:T(8,128)(2,1)S(1)} %add.19.refs_0_), channel_id=1, source_target_pairs={{0,10},{1,11},{2,8},{3,9},{4,14},{5,15},{6,12},{7,13},{8,2},{9,3},... | collective-permute-start | bytes 196616 | tf_op jit(solution)/shard_map/ppermute | solution.py:262
  25.8 2.7 %collective-permute-done.3.refs_2_ = bf16[128,256]{1,0:T(8,128)(2,1)S(1)} collective-permute-done((bf16[128,256]{1,0:T(8,128)(2,1)S(1)}, bf16[128,256]{1,0:T(8,128)(2,1)S(1)}, u32[]{:S(2)}, u32[]{:S(2)}) %collective-permute-start.3) | collective-permute-done | bytes 65568 | tf_op jit(solution)/shard_map/ppermute | solution.py:262
  29.4 3.9 %all-gather = bf16[256,256]{1,0:T(8,128)(2,1)S(1)} all-gather(bf16[128,256]{1,0:T(8,128)(2,1)S(1)} %add.20), channel_id=2, replica_groups={{0,1},{2,3},{4,5},{6,7},{8,9},{10,11},{12,13},{14,15},{16,17},{18,19},{..., dimensions={0}, use_global_device_ids=true | all-gather | bytes 196608 | tf_op jit(solution)/shard_map/all_gather | solution.py:282
  33.4 2.7 %first_step.2 = (f32[256,256]{1,0:T(8,128)S(1)}, bf16[128,256]{1,0:T(8,128)(2,1)S(1)}, bf16[128,256]{1,0:T(8,128)(2,1)S(1)}, f32[256,256]{1,0:T(8,128)S(1)}) custom-call(s32[1,2]{1,0:T(1,128)S(1)} %copy-done.5, f32[256,256]{1,0:T(8,128)S(1)} %get-tuple-element.29.vector, f32[256,256]{1,0:T(8,128)S(1)} %get-tuple-element.30.applied, ...), custom_call_target="tpu_custom_call" | custom-call | flops 1677721600 | bytes 6553600 | tf_op jit(solution)/shard_map/first_step/pallas_call | solution.py:259
  37.4 2.2 %collective-permute-start.6 = (bf16[128,256]{1,0:T(8,128)(2,1)S(1)}, bf16[128,256]{1,0:T(8,128)(2,1)S(1)}, u32[]{:S(2)}, u32[]{:S(2)}) collective-permute-start(bf16[128,256]{1,0:T(8,128)(2,1)S(1)} %add.21.refs_0_), channel_id=1, source_target_pairs={{0,2},{1,3},{2,0},{3,1},{4,6},{5,7},{6,4},{7,5},{8,10},{9,11},{10,... | collective-permute-start | bytes 196616 | tf_op jit(solution)/shard_map/ppermute | solution.py:262
  39.7 2.2 %collective-permute-done.6.refs_1_ = bf16[128,256]{1,0:T(8,128)(2,1)S(1)} collective-permute-done((bf16[128,256]{1,0:T(8,128)(2,1)S(1)}, bf16[128,256]{1,0:T(8,128)(2,1)S(1)}, u32[]{:S(2)}, u32[]{:S(2)}) %collective-permute-start.6) | collective-permute-done | bytes 65568 | tf_op jit(solution)/shard_map/ppermute | solution.py:262
  41.9 2.4 %collective-permute-start.9 = (bf16[128,256]{1,0:T(8,128)(2,1)S(1)}, bf16[128,256]{1,0:T(8,128)(2,1)S(1)}, u32[]{:S(2)}, u32[]{:S(2)}) collective-permute-start(bf16[128,256]{1,0:T(8,128)(2,1)S(1)} %add.22.refs_0_), channel_id=1, source_target_pairs={{0,10},{1,11},{2,8},{3,9},{4,14},{5,15},{6,12},{7,13},{8,2},{9,3},... | collective-permute-start | bytes 196616 | tf_op jit(solution)/shard_map/ppermute | solution.py:262
  50.8 4.2 %all-gather.1 = bf16[256,256]{1,0:T(8,128)(2,1)S(1)} all-gather(bf16[128,256]{1,0:T(8,128)(2,1)S(1)} %add.23), channel_id=3, replica_groups={{0,1},{2,3},{4,5},{6,7},{8,9},{10,11},{12,13},{14,15},{16,17},{18,19},{..., dimensions={0}, use_global_device_ids=true | all-gather | bytes 196608 | tf_op jit(solution)/shard_map/all_gather | solution.py:282
  55.0 2.7 %first_step.3 = (f32[256,256]{1,0:T(8,128)S(1)}, bf16[128,256]{1,0:T(8,128)(2,1)S(1)}, bf16[128,256]{1,0:T(8,128)(2,1)S(1)}) custom-call(s32[1,2]{1,0:T(1,128)S(1)} %copy-done.5, f32[256,256]{1,0:T(8,128)S(1)} %get-tuple-element.33.vector, f32[256,256]{1,0:T(8,128)S(1)} %get-tuple-element.34.applied, bf16[2,128,256]{2,1,0:T(8,128)(2,1)S(1)} %bitcast.10, ...), custom_call_target="tpu_custom_call" | custom-call | flops 1677721600 | bytes 6553600 | tf_op jit(solution)/shard_map/first_step/pallas_call | solution.py:259
  60.1 2.1 %collective-permute-done.11.refs_1_ = bf16[128,256]{1,0:T(8,128)(2,1)S(1)} collective-permute-done((bf16[128,256]{1,0:T(8,128)(2,1)S(1)}, bf16[128,256]{1,0:T(8,128)(2,1)S(1)}, u32[]{:S(2)}, u32[]{:S(2)}) %collective-permute-start.11) | collective-permute-done | bytes 65568 | tf_op jit(solution)/shard_map/ppermute | solution.py:262
  62.3 2.5 %collective-permute-start.14 = (bf16[128,256]{1,0:T(8,128)(2,1)S(1)}, bf16[128,256]{1,0:T(8,128)(2,1)S(1)}, u32[]{:S(2)}, u32[]{:S(2)}) collective-permute-start(bf16[128,256]{1,0:T(8,128)(2,1)S(1)} %add.25.refs_0_), channel_id=1, source_target_pairs={{0,10},{1,11},{2,8},{3,9},{4,14},{5,15},{6,12},{7,13},{8,2},{9,3},... | collective-permute-start | bytes 196616 | tf_op jit(solution)/shard_map/ppermute | solution.py:262
  69.4 2.3 %collective-permute-done.12.refs_1_ = bf16[128,256]{1,0:T(8,128)(2,1)S(1)} collective-permute-done((bf16[128,256]{1,0:T(8,128)(2,1)S(1)}, bf16[128,256]{1,0:T(8,128)(2,1)S(1)}, u32[]{:S(2)}, u32[]{:S(2)}) %collective-permute-start.12) | collective-permute-done | bytes 65568 | tf_op jit(solution)/shard_map/ppermute | solution.py:262
  71.7 3.4 %all-gather.2 = bf16[256,256]{1,0:T(8,128)(2,1)S(1)} all-gather(bf16[128,256]{1,0:T(8,128)(2,1)S(1)} %add.26), channel_id=4, replica_groups={{0,1},{2,3},{4,5},{6,7},{8,9},{10,11},{12,13},{14,15},{16,17},{18,19},{..., dimensions={0}, use_global_device_ids=true | all-gather | bytes 196608 | tf_op jit(solution)/shard_map/all_gather | solution.py:282
  75.2 3.5 %second_start.1 = (f32[1,16,256]{2,1,0:T(8,128)}, bf16[256,256]{1,0:T(8,128)(2,1)S(1)}, bf16[128,256]{1,0:T(8,128)(2,1)S(1)}, bf16[128,256]{1,0:T(8,128)(2,1)S(1)}, f32[256,256]{1,0:T(8,128)S(1)}) custom-call(s32[1,2]{1,0:T(1,128)S(1)} %copy-done.5, f32[256,256]{1,0:T(8,128)S(1)} %get-tuple-element.37.vector, bf16[2,128,256]{2,1,0:T(8,128)(2,1)S(1)} %bitcast.7, ...), custom_call_target="tpu_custom_call" | custom-call | flops 1677721600 | bytes 6553600 | tf_op jit(solution)/shard_map/second_start/pallas_call | solution.py:317
  81.2 2.1 %collective-permute-done.17.refs_1_ = bf16[128,256]{1,0:T(8,128)(2,1)S(1)} collective-permute-done((bf16[128,256]{1,0:T(8,128)(2,1)S(1)}, bf16[128,256]{1,0:T(8,128)(2,1)S(1)}, u32[]{:S(2)}, u32[]{:S(2)}) %collective-permute-start.17) | collective-permute-done | bytes 65568 | tf_op jit(solution)/shard_map/ppermute | solution.py:262
  83.2 2.6 %collective-permute-start.20 = (bf16[128,256]{1,0:T(8,128)(2,1)S(1)}, bf16[128,256]{1,0:T(8,128)(2,1)S(1)}, u32[]{:S(2)}, u32[]{:S(2)}) collective-permute-start(bf16[128,256]{1,0:T(8,128)(2,1)S(1)} %add.28.refs_0_), channel_id=1, source_target_pairs={{0,10},{1,11},{2,8},{3,9},{4,14},{5,15},{6,12},{7,13},{8,2},{9,3},... | collective-permute-start | bytes 196616 | tf_op jit(solution)/shard_map/ppermute | solution.py:262
  90.4 2.4 %collective-permute-done.18.refs_1_ = bf16[128,256]{1,0:T(8,128)(2,1)S(1)} collective-permute-done((bf16[128,256]{1,0:T(8,128)(2,1)S(1)}, bf16[128,256]{1,0:T(8,128)(2,1)S(1)}, u32[]{:S(2)}, u32[]{:S(2)}) %collective-permute-start.18) | collective-permute-done | bytes 65568 | tf_op jit(solution)/shard_map/ppermute | solution.py:262
  92.8 3.4 %all-gather.3 = bf16[256,256]{1,0:T(8,128)(2,1)S(1)} all-gather(bf16[128,256]{1,0:T(8,128)(2,1)S(1)} %add.29), channel_id=5, replica_groups={{0,1},{2,3},{4,5},{6,7},{8,9},{10,11},{12,13},{14,15},{16,17},{18,19},{..., dimensions={0}, use_global_device_ids=true | all-gather | bytes 196608 | tf_op jit(solution)/shard_map/all_gather | solution.py:282
  96.2 3.4 %second_step.2 = (f32[256,256]{1,0:T(8,128)S(1)}, bf16[128,256]{1,0:T(8,128)(2,1)S(1)}, bf16[128,256]{1,0:T(8,128)(2,1)S(1)}, f32[256,256]{1,0:T(8,128)S(1)}) custom-call(s32[1,2]{1,0:T(1,128)S(1)} %copy-done.5, f32[256,256]{1,0:T(8,128)S(1)} %get-tuple-element.44.vector, f32[256,256]{1,0:T(8,128)S(1)} %get-tuple-element.45.applied, ...), custom_call_target="tpu_custom_call" | custom-call | flops 1677721600 | bytes 6553600 | tf_op jit(solution)/shard_map/second_step/pallas_call | solution.py:259
  102.1 2.0 %collective-permute-done.22.refs_1_ = bf16[128,256]{1,0:T(8,128)(2,1)S(1)} collective-permute-done((bf16[128,256]{1,0:T(8,128)(2,1)S(1)}, bf16[128,256]{1,0:T(8,128)(2,1)S(1)}, u32[]{:S(2)}, u32[]{:S(2)}) %collective-permute-start.22) | collective-permute-done | bytes 65568 | tf_op jit(solution)/shard_map/ppermute | solution.py:262
  104.1 2.6 %collective-permute-start.25 = (bf16[128,256]{1,0:T(8,128)(2,1)S(1)}, bf16[128,256]{1,0:T(8,128)(2,1)S(1)}, u32[]{:S(2)}, u32[]{:S(2)}) collective-permute-start(bf16[128,256]{1,0:T(8,128)(2,1)S(1)} %add.31.refs_0_), channel_id=1, source_target_pairs={{0,10},{1,11},{2,8},{3,9},{4,14},{5,15},{6,12},{7,13},{8,2},{9,3},... | collective-permute-start | bytes 196616 | tf_op jit(solution)/shard_map/ppermute | solution.py:262
  111.3 2.3 %collective-permute-done.23.refs_1_ = bf16[128,256]{1,0:T(8,128)(2,1)S(1)} collective-permute-done((bf16[128,256]{1,0:T(8,128)(2,1)S(1)}, bf16[128,256]{1,0:T(8,128)(2,1)S(1)}, u32[]{:S(2)}, u32[]{:S(2)}) %collective-permute-start.23) | collective-permute-done | bytes 65568 | tf_op jit(solution)/shard_map/ppermute | solution.py:262
  113.6 3.4 %all-gather.4 = bf16[256,256]{1,0:T(8,128)(2,1)S(1)} all-gather(bf16[128,256]{1,0:T(8,128)(2,1)S(1)} %add.32), channel_id=6, replica_groups={{0,1},{2,3},{4,5},{6,7},{8,9},{10,11},{12,13},{14,15},{16,17},{18,19},{..., dimensions={0}, use_global_device_ids=true | all-gather | bytes 196608 | tf_op jit(solution)/shard_map/all_gather | solution.py:282
  117.1 3.4 %second_step.3 = (f32[256,256]{1,0:T(8,128)S(1)}, bf16[128,256]{1,0:T(8,128)(2,1)S(1)}, bf16[128,256]{1,0:T(8,128)(2,1)S(1)}) custom-call(s32[1,2]{1,0:T(1,128)S(1)} %copy-done.5, f32[256,256]{1,0:T(8,128)S(1)} %get-tuple-element.49.vector, f32[256,256]{1,0:T(8,128)S(1)} %get-tuple-element.50.applied, bf16[2,128,256]{2,1,0:T(8,128)(2,1)S(1)} %bitcast.6, ...), custom_call_target="tpu_custom_call" | custom-call | flops 1677721600 | bytes 6553600 | tf_op jit(solution)/shard_map/second_step/pallas_call | solution.py:259
  123.0 2.0 %collective-permute-done.27.refs_1_ = bf16[128,256]{1,0:T(8,128)(2,1)S(1)} collective-permute-done((bf16[128,256]{1,0:T(8,128)(2,1)S(1)}, bf16[128,256]{1,0:T(8,128)(2,1)S(1)}, u32[]{:S(2)}, u32[]{:S(2)}) %collective-permute-start.27) | collective-permute-done | bytes 65568 | tf_op jit(solution)/shard_map/ppermute | solution.py:262
  125.0 2.6 %collective-permute-start.30 = (bf16[128,256]{1,0:T(8,128)(2,1)S(1)}, bf16[128,256]{1,0:T(8,128)(2,1)S(1)}, u32[]{:S(2)}, u32[]{:S(2)}) collective-permute-start(bf16[128,256]{1,0:T(8,128)(2,1)S(1)} %add.34.refs_0_), channel_id=1, source_target_pairs={{0,10},{1,11},{2,8},{3,9},{4,14},{5,15},{6,12},{7,13},{8,2},{9,3},... | collective-permute-start | bytes 196616 | tf_op jit(solution)/shard_map/ppermute | solution.py:262
  132.2 2.4 %collective-permute-done.28.refs_1_ = bf16[128,256]{1,0:T(8,128)(2,1)S(1)} collective-permute-done((bf16[128,256]{1,0:T(8,128)(2,1)S(1)}, bf16[128,256]{1,0:T(8,128)(2,1)S(1)}, u32[]{:S(2)}, u32[]{:S(2)}) %collective-permute-start.28) | collective-permute-done | bytes 65568 | tf_op jit(solution)/shard_map/ppermute | solution.py:262
  134.6 3.4 %all-gather.5 = bf16[256,256]{1,0:T(8,128)(2,1)S(1)} all-gather(bf16[128,256]{1,0:T(8,128)(2,1)S(1)} %add.35), channel_id=7, replica_groups={{0,1},{2,3},{4,5},{6,7},{8,9},{10,11},{12,13},{14,15},{16,17},{18,19},{..., dimensions={0}, use_global_device_ids=true | all-gather | bytes 196608 | tf_op jit(solution)/shard_map/all_gather | solution.py:282
  (81 shorter events, 46.9 us)
Async XLA Ops:
  5.5 61.6 %collective-permute-start.15 = (bf16[3776,256]{1,0:T(8,128)(2,1)S(1)}, bf16[3776,256]{1,0:T(8,128)(2,1)S(1)}, u32[]{:S(2)}, u32[]{:S(2)}) collective-permute-start(bf16[3776,256]{1,0:T(8,128)(2,1)S(1)} %pack.1), channel_id=1, source_target_pairs={{0,16},{16,32},{32,48},{48,64},{64,80},{80,96},{96,112},{112,128},... | collective-permute-start | bytes 5799944 | tf_op jit(solution)/shard_map/ppermute | solution.py:297
  12.3 1.9 %collective-permute-start = (bf16[128,256]{1,0:T(8,128)(2,1)S(1)}, bf16[128,256]{1,0:T(8,128)(2,1)S(1)}, u32[]{:S(2)}, u32[]{:S(2)}) collective-permute-start(bf16[128,256]{1,0:T(8,128)(2,1)S(1)} %get-tuple-element.32), channel_id=1, source_target_pairs={{0,1},{1,0},{2,3},{3,2},{4,5},{5,4},{6,7},{7,6},{8,9},{9,8},{10,11... | collective-permute-start | bytes 196616 | tf_op jit(solution)/shard_map/ppermute | solution.py:262
  14.2 3.8 %collective-permute-start.1 = (bf16[128,256]{1,0:T(8,128)(2,1)S(1)}, bf16[128,256]{1,0:T(8,128)(2,1)S(1)}, u32[]{:S(2)}, u32[]{:S(2)}) collective-permute-start(bf16[128,256]{1,0:T(8,128)(2,1)S(1)} %add.18.refs_0_), channel_id=1, source_target_pairs={{0,2},{1,3},{2,0},{3,1},{4,6},{5,7},{6,4},{7,5},{8,10},{9,11},{10,... | collective-permute-start | bytes 196616 | tf_op jit(solution)/shard_map/ppermute | solution.py:262
  18.1 7.7 %collective-permute-start.4 = (bf16[128,256]{1,0:T(8,128)(2,1)S(1)}, bf16[128,256]{1,0:T(8,128)(2,1)S(1)}, u32[]{:S(2)}, u32[]{:S(2)}) collective-permute-start(bf16[128,256]{1,0:T(8,128)(2,1)S(1)} %add.19.refs_0_), channel_id=1, source_target_pairs={{0,10},{1,11},{2,8},{3,9},{4,14},{5,15},{6,12},{7,13},{8,2},{9,3},... | collective-permute-start | bytes 196616 | tf_op jit(solution)/shard_map/ppermute | solution.py:262
  24.0 4.5 %collective-permute-start.3 = (bf16[128,256]{1,0:T(8,128)(2,1)S(1)}, bf16[128,256]{1,0:T(8,128)(2,1)S(1)}, u32[]{:S(2)}, u32[]{:S(2)}) collective-permute-start(bf16[128,256]{1,0:T(8,128)(2,1)S(1)} %add.19.refs_0_), channel_id=1, source_target_pairs={{0,14},{1,15},{2,4},{3,5},{4,2},{5,3},{6,8},{7,9},{8,6},{9,7},{10,... | collective-permute-start | bytes 196616 | tf_op jit(solution)/shard_map/ppermute | solution.py:262
  24.0 5.4 %collective-permute-start.2 = (bf16[128,256]{1,0:T(8,128)(2,1)S(1)}, bf16[128,256]{1,0:T(8,128)(2,1)S(1)}, u32[]{:S(2)}, u32[]{:S(2)}) collective-permute-start(bf16[128,256]{1,0:T(8,128)(2,1)S(1)} %add.19.refs_0_), channel_id=1, source_target_pairs={{0,12},{1,13},{2,6},{3,7},{4,0},{5,1},{6,10},{7,11},{8,4},{9,5},{1... | collective-permute-start | bytes 196616 | tf_op jit(solution)/shard_map/ppermute | solution.py:262
  36.1 1.3 collective-permute-start.5
  37.4 4.4 %collective-permute-start.6 = (bf16[128,256]{1,0:T(8,128)(2,1)S(1)}, bf16[128,256]{1,0:T(8,128)(2,1)S(1)}, u32[]{:S(2)}, u32[]{:S(2)}) collective-permute-start(bf16[128,256]{1,0:T(8,128)(2,1)S(1)} %add.21.refs_0_), channel_id=1, source_target_pairs={{0,2},{1,3},{2,0},{3,1},{4,6},{5,7},{6,4},{7,5},{8,10},{9,11},{10,... | collective-permute-start | bytes 196616 | tf_op jit(solution)/shard_map/ppermute | solution.py:262
  41.9 6.2 %collective-permute-start.9 = (bf16[128,256]{1,0:T(8,128)(2,1)S(1)}, bf16[128,256]{1,0:T(8,128)(2,1)S(1)}, u32[]{:S(2)}, u32[]{:S(2)}) collective-permute-start(bf16[128,256]{1,0:T(8,128)(2,1)S(1)} %add.22.refs_0_), channel_id=1, source_target_pairs={{0,10},{1,11},{2,8},{3,9},{4,14},{5,15},{6,12},{7,13},{8,2},{9,3},... | collective-permute-start | bytes 196616 | tf_op jit(solution)/shard_map/ppermute | solution.py:262
  44.3 5.3 %collective-permute-start.8 = (bf16[128,256]{1,0:T(8,128)(2,1)S(1)}, bf16[128,256]{1,0:T(8,128)(2,1)S(1)}, u32[]{:S(2)}, u32[]{:S(2)}) collective-permute-start(bf16[128,256]{1,0:T(8,128)(2,1)S(1)} %add.22.refs_0_), channel_id=1, source_target_pairs={{0,14},{1,15},{2,4},{3,5},{4,2},{5,3},{6,8},{7,9},{8,6},{9,7},{10,... | collective-permute-start | bytes 196616 | tf_op jit(solution)/shard_map/ppermute | solution.py:262
  45.7 5.0 %collective-permute-start.7 = (bf16[128,256]{1,0:T(8,128)(2,1)S(1)}, bf16[128,256]{1,0:T(8,128)(2,1)S(1)}, u32[]{:S(2)}, u32[]{:S(2)}) collective-permute-start(bf16[128,256]{1,0:T(8,128)(2,1)S(1)} %add.22.refs_0_), channel_id=1, source_target_pairs={{0,12},{1,13},{2,6},{3,7},{4,0},{5,1},{6,10},{7,11},{8,4},{9,5},{1... | collective-permute-start | bytes 196616 | tf_op jit(solution)/shard_map/ppermute | solution.py:262
  55.0 12.2 %copy-start.7 = (f32[1,25]{1,0:T(1,128)S(1)}, f32[1,25]{1,0:T(1,128)}, u32[]{:S(2)}) copy-start(f32[1,25]{1,0:T(1,128)} %gain.3) | copy-start | bytes 304
  57.7 1.3 collective-permute-start.10
  59.0 3.2 %collective-permute-start.11 = (bf16[128,256]{1,0:T(8,128)(2,1)S(1)}, bf16[128,256]{1,0:T(8,128)(2,1)S(1)}, u32[]{:S(2)}, u32[]{:S(2)}) collective-permute-start(bf16[128,256]{1,0:T(8,128)(2,1)S(1)} %add.24.refs_0_), channel_id=1, source_target_pairs={{0,2},{1,3},{2,0},{3,1},{4,6},{5,7},{6,4},{7,5},{8,10},{9,11},{10,... | collective-permute-start | bytes 196616 | tf_op jit(solution)/shard_map/ppermute | solution.py:262
  62.3 6.4 %collective-permute-start.14 = (bf16[128,256]{1,0:T(8,128)(2,1)S(1)}, bf16[128,256]{1,0:T(8,128)(2,1)S(1)}, u32[]{:S(2)}, u32[]{:S(2)}) collective-permute-start(bf16[128,256]{1,0:T(8,128)(2,1)S(1)} %add.25.refs_0_), channel_id=1, source_target_pairs={{0,10},{1,11},{2,8},{3,9},{4,14},{5,15},{6,12},{7,13},{8,2},{9,3},... | collective-permute-start | bytes 196616 | tf_op jit(solution)/shard_map/ppermute | solution.py:262
  64.8 4.6 %collective-permute-start.13 = (bf16[128,256]{1,0:T(8,128)(2,1)S(1)}, bf16[128,256]{1,0:T(8,128)(2,1)S(1)}, u32[]{:S(2)}, u32[]{:S(2)}) collective-permute-start(bf16[128,256]{1,0:T(8,128)(2,1)S(1)} %add.25.refs_0_), channel_id=1, source_target_pairs={{0,14},{1,15},{2,4},{3,5},{4,2},{5,3},{6,8},{7,9},{8,6},{9,7},{10,... | collective-permute-start | bytes 196616 | tf_op jit(solution)/shard_map/ppermute | solution.py:262
  66.2 5.5 %collective-permute-start.12 = (bf16[128,256]{1,0:T(8,128)(2,1)S(1)}, bf16[128,256]{1,0:T(8,128)(2,1)S(1)}, u32[]{:S(2)}, u32[]{:S(2)}) collective-permute-start(bf16[128,256]{1,0:T(8,128)(2,1)S(1)} %add.25.refs_0_), channel_id=1, source_target_pairs={{0,12},{1,13},{2,6},{3,7},{4,0},{5,1},{6,10},{7,11},{8,4},{9,5},{1... | collective-permute-start | bytes 196616 | tf_op jit(solution)/shard_map/ppermute | solution.py:262
  78.7 1.3 collective-permute-start.16
  80.0 3.2 %collective-permute-start.17 = (bf16[128,256]{1,0:T(8,128)(2,1)S(1)}, bf16[128,256]{1,0:T(8,128)(2,1)S(1)}, u32[]{:S(2)}, u32[]{:S(2)}) collective-permute-start(bf16[128,256]{1,0:T(8,128)(2,1)S(1)} %add.27.refs_0_), channel_id=1, source_target_pairs={{0,2},{1,3},{2,0},{3,1},{4,6},{5,7},{6,4},{7,5},{8,10},{9,11},{10,... | collective-permute-start | bytes 196616 | tf_op jit(solution)/shard_map/ppermute | solution.py:262
  83.2 6.3 %collective-permute-start.20 = (bf16[128,256]{1,0:T(8,128)(2,1)S(1)}, bf16[128,256]{1,0:T(8,128)(2,1)S(1)}, u32[]{:S(2)}, u32[]{:S(2)}) collective-permute-start(bf16[128,256]{1,0:T(8,128)(2,1)S(1)} %add.28.refs_0_), channel_id=1, source_target_pairs={{0,10},{1,11},{2,8},{3,9},{4,14},{5,15},{6,12},{7,13},{8,2},{9,3},... | collective-permute-start | bytes 196616 | tf_op jit(solution)/shard_map/ppermute | solution.py:262
  85.8 4.5 %collective-permute-start.19 = (bf16[128,256]{1,0:T(8,128)(2,1)S(1)}, bf16[128,256]{1,0:T(8,128)(2,1)S(1)}, u32[]{:S(2)}, u32[]{:S(2)}) collective-permute-start(bf16[128,256]{1,0:T(8,128)(2,1)S(1)} %add.28.refs_0_), channel_id=1, source_target_pairs={{0,14},{1,15},{2,4},{3,5},{4,2},{5,3},{6,8},{7,9},{8,6},{9,7},{10,... | collective-permute-start | bytes 196616 | tf_op jit(solution)/shard_map/ppermute | solution.py:262
  87.2 5.5 %collective-permute-start.18 = (bf16[128,256]{1,0:T(8,128)(2,1)S(1)}, bf16[128,256]{1,0:T(8,128)(2,1)S(1)}, u32[]{:S(2)}, u32[]{:S(2)}) collective-permute-start(bf16[128,256]{1,0:T(8,128)(2,1)S(1)} %add.28.refs_0_), channel_id=1, source_target_pairs={{0,12},{1,13},{2,6},{3,7},{4,0},{5,1},{6,10},{7,11},{8,4},{9,5},{1... | collective-permute-start | bytes 196616 | tf_op jit(solution)/shard_map/ppermute | solution.py:262
  99.5 1.3 collective-permute-start.21
  100.9 3.2 %collective-permute-start.22 = (bf16[128,256]{1,0:T(8,128)(2,1)S(1)}, bf16[128,256]{1,0:T(8,128)(2,1)S(1)}, u32[]{:S(2)}, u32[]{:S(2)}) collective-permute-start(bf16[128,256]{1,0:T(8,128)(2,1)S(1)} %add.30.refs_0_), channel_id=1, source_target_pairs={{0,2},{1,3},{2,0},{3,1},{4,6},{5,7},{6,4},{7,5},{8,10},{9,11},{10,... | collective-permute-start | bytes 196616 | tf_op jit(solution)/shard_map/ppermute | solution.py:262
  104.1 6.3 %collective-permute-start.25 = (bf16[128,256]{1,0:T(8,128)(2,1)S(1)}, bf16[128,256]{1,0:T(8,128)(2,1)S(1)}, u32[]{:S(2)}, u32[]{:S(2)}) collective-permute-start(bf16[128,256]{1,0:T(8,128)(2,1)S(1)} %add.31.refs_0_), channel_id=1, source_target_pairs={{0,10},{1,11},{2,8},{3,9},{4,14},{5,15},{6,12},{7,13},{8,2},{9,3},... | collective-permute-start | bytes 196616 | tf_op jit(solution)/shard_map/ppermute | solution.py:262
  106.7 4.5 %collective-permute-start.24 = (bf16[128,256]{1,0:T(8,128)(2,1)S(1)}, bf16[128,256]{1,0:T(8,128)(2,1)S(1)}, u32[]{:S(2)}, u32[]{:S(2)}) collective-permute-start(bf16[128,256]{1,0:T(8,128)(2,1)S(1)} %add.31.refs_0_), channel_id=1, source_target_pairs={{0,14},{1,15},{2,4},{3,5},{4,2},{5,3},{6,8},{7,9},{8,6},{9,7},{10,... | collective-permute-start | bytes 196616 | tf_op jit(solution)/shard_map/ppermute | solution.py:262
  108.1 5.5 %collective-permute-start.23 = (bf16[128,256]{1,0:T(8,128)(2,1)S(1)}, bf16[128,256]{1,0:T(8,128)(2,1)S(1)}, u32[]{:S(2)}, u32[]{:S(2)}) collective-permute-start(bf16[128,256]{1,0:T(8,128)(2,1)S(1)} %add.31.refs_0_), channel_id=1, source_target_pairs={{0,12},{1,13},{2,6},{3,7},{4,0},{5,1},{6,10},{7,11},{8,4},{9,5},{1... | collective-permute-start | bytes 196616 | tf_op jit(solution)/shard_map/ppermute | solution.py:262
  120.4 1.3 collective-permute-start.26
  121.8 3.2 %collective-permute-start.27 = (bf16[128,256]{1,0:T(8,128)(2,1)S(1)}, bf16[128,256]{1,0:T(8,128)(2,1)S(1)}, u32[]{:S(2)}, u32[]{:S(2)}) collective-permute-start(bf16[128,256]{1,0:T(8,128)(2,1)S(1)} %add.33.refs_0_), channel_id=1, source_target_pairs={{0,2},{1,3},{2,0},{3,1},{4,6},{5,7},{6,4},{7,5},{8,10},{9,11},{10,... | collective-permute-start | bytes 196616 | tf_op jit(solution)/shard_map/ppermute | solution.py:262
  125.0 6.3 %collective-permute-start.30 = (bf16[128,256]{1,0:T(8,128)(2,1)S(1)}, bf16[128,256]{1,0:T(8,128)(2,1)S(1)}, u32[]{:S(2)}, u32[]{:S(2)}) collective-permute-start(bf16[128,256]{1,0:T(8,128)(2,1)S(1)} %add.34.refs_0_), channel_id=1, source_target_pairs={{0,10},{1,11},{2,8},{3,9},{4,14},{5,15},{6,12},{7,13},{8,2},{9,3},... | collective-permute-start | bytes 196616 | tf_op jit(solution)/shard_map/ppermute | solution.py:262
  127.6 4.5 %collective-permute-start.29 = (bf16[128,256]{1,0:T(8,128)(2,1)S(1)}, bf16[128,256]{1,0:T(8,128)(2,1)S(1)}, u32[]{:S(2)}, u32[]{:S(2)}) collective-permute-start(bf16[128,256]{1,0:T(8,128)(2,1)S(1)} %add.34.refs_0_), channel_id=1, source_target_pairs={{0,14},{1,15},{2,4},{3,5},{4,2},{5,3},{6,8},{7,9},{8,6},{9,7},{10,... | collective-permute-start | bytes 196616 | tf_op jit(solution)/shard_map/ppermute | solution.py:262
  129.0 5.5 %collective-permute-start.28 = (bf16[128,256]{1,0:T(8,128)(2,1)S(1)}, bf16[128,256]{1,0:T(8,128)(2,1)S(1)}, u32[]{:S(2)}, u32[]{:S(2)}) collective-permute-start(bf16[128,256]{1,0:T(8,128)(2,1)S(1)} %add.34.refs_0_), channel_id=1, source_target_pairs={{0,12},{1,13},{2,6},{3,7},{4,0},{5,1},{6,10},{7,11},{8,4},{9,5},{1... | collective-permute-start | bytes 196616 | tf_op jit(solution)/shard_map/ppermute | solution.py:262
  (8 other events, 40.6 us)

commit v2 on v1

--- a/solution.py
+++ b/solution.py
@@ -71,10 +71,10 @@
     chunk = CHUNK if terms % CHUNK == 0 else 1
     for first in range(0, terms, chunk):
         inner = dot(left[first : first + chunk].reshape(chunk * states, states), vector)
-        total = None
-        for n in range(chunk):
-            part = dot(inner[n * states : (n + 1) * states].astype(BF16), right[first + n])
-            total = part if total is None else total + part
+        inner = inner.astype(BF16)
+        inner = [inner[n * states : (n + 1) * states] for n in range(chunk)]
+        outer = right[first : first + chunk].reshape(chunk * states, states)
+        total = dot(jnp.concatenate(inner, axis=1), outer)
         if first == 0:
             acc[...] = total
         else:
@@ -113,7 +113,11 @@
     return lax.broadcasted_iota(jnp.int32, shape, 0), lax.broadcasted_iota(jnp.int32, shape, 1)
 
 
-def pack(gain, left, edge, package):
+def wake(ready):
+    ready[...] = jnp.zeros_like(ready)
+
+
+def pack(gain, left, edge, ready, package):
     terms, states = left.shape[1], left.shape[2]
     row, column = place((states, states))
     pairs = terms // 2
@@ -285,15 +289,17 @@
     blocks = shape(terms, states, states)
     left, right = left_env, right_env
     slabs = terms // 2 + terms % 2 + 1
+    shadow = pl.CostEstimate(
+        flops=60 * terms * states**3, bytes_accessed=4 * terms * states**2, transcendentals=0
+    )
+    (ready,) = call(wake, [], [shape(8, 128, dtype=F32)], (), MIB, shadow)()
     (package,) = call(
         pack,
-        [smem, vmem, vmem],
+        [smem, vmem, vmem, vmem],
         [shape(slabs * states + 16 * (terms // 2), states)],
         (),
-        cost=pl.CostEstimate(
-            flops=60 * terms * states**3, bytes_accessed=4 * terms * states**2, transcendentals=0
-        ),
-    )(mpo_gain, left_env, edge_site)
+        cost=shadow,
+    )(mpo_gain, left_env, edge_site, ready)
     package = lax.ppermute(package, "seg", [(n, n + 1) for n in range(segments - 1)])
 
     vector, mine, theirs, *applied = call(

time: 140 us -> 137 us (0.979)
  local copies, waits for them, and re-layouts: 3.65 us -> 1.92 us
    unnamed x18 -> x14, local copies, waits for them, and re-layouts: 3.65 us -> 1.92 us
where the time goes in v2:
time: 137 us
  starting transfers between devices  46.4 us (34%)
  waiting for transfers between devices  43.8 us (32%)
  Pallas kernels  22.5 us (16%)
  blocking collectives  21.8 us (16%)
  local copies, waits for them, and re-layouts  1.92 us (1%)
    ppermute x30, waiting for transfers between devices, moved(): lax.ppermute(value, 'sec', [(n, target(n) % sections) for n in range(sect...  43.8 us
    ppermute x30, starting transfers between devices, moved(): lax.ppermute(value, 'sec', [(n, target(n) % sections) for n in range(sect...  42.3 us
    all_gather x6, blocking collectives, summed(): return (lax.all_gather(total, 'sec', axis=0, axis_index_groups=cores),)  21.8 us
    pallas_call x4, Pallas kernels, step_call(): call(kernel, specs, outs, scratch, cost=apply_cost)  11.8 us
    ppermute x1, starting transfers between devices, on_device(): lax.ppermute(package, 'seg', [(n, n + 1) for n in range(segments - 1)])  4.07 us
    pallas_call x1, Pallas kernels, on_device(): call(second_start, [smem, vmem, tuple((vmem for _ in total)), *[vmem] * 4...  3.42 us
  transfers between devices with their start and end apart: 31, of which 29 were waited for; matrix products, arithmetic and copies ran while one was open for 0% of the time, Pallas kernels for 7%

profile of v2, /device:TPU:1, one launch (start us, length us, event | category | flops | bytes accessed | tf_op | source)
XLA Modules:
  0.0 137.2 jit_solution(13512833195005404350)
XLA Ops:
  0.7 1.9 %copy-done.1 = bf16[1,25,256,256]{3,2,1,0:T(8,128)(2,1)S(1)} copy-done((bf16[1,25,256,256]{3,2,1,0:T(8,128)(2,1)S(1)}, bf16[1,25,256,256]{3,2,1,0:T(8,128)(2,1)}, u32[]{:S(2)}) %copy-start.1) | copy-done | bytes 3276824
  3.8 4.1 %collective-permute-start.15 = (bf16[3776,256]{1,0:T(8,128)(2,1)S(1)}, bf16[3776,256]{1,0:T(8,128)(2,1)S(1)}, u32[]{:S(2)}, u32[]{:S(2)}) collective-permute-start(bf16[3776,256]{1,0:T(8,128)(2,1)S(1)} %pack.1), channel_id=1, source_target_pairs={{0,16},{16,32},{32,48},{48,64},{64,80},{80,96},{96,112},{112,128},... | collective-permute-start | bytes 5799944 | tf_op jit(solution)/shard_map/ppermute | solution.py:303
  7.9 2.6 %first_start.1 = (f32[256,256]{1,0:T(8,128)S(1)}, bf16[128,256]{1,0:T(8,128)(2,1)S(1)}, bf16[128,256]{1,0:T(8,128)(2,1)S(1)}, f32[256,256]{1,0:T(8,128)S(1)}) custom-call(s32[1,2]{1,0:T(1,128)S(1)} %copy-done.4, bf16[1,256,256]{2,1,0:T(8,128)(2,1)S(1)} %copy-done.2, bf16[1,25,256,256]{3,2,1,0:T(8,128)(2,1)S(1)} %copy-done.1, ...), custom_call_target="tpu_custom_call" | custom-call | flops 1677721600 | bytes 6553600 | tf_op jit(solution)/shard_map/first_start/pallas_call | solution.py:305
  14.2 2.1 %collective-permute-done.1.refs_1_ = bf16[128,256]{1,0:T(8,128)(2,1)S(1)} collective-permute-done((bf16[128,256]{1,0:T(8,128)(2,1)S(1)}, bf16[128,256]{1,0:T(8,128)(2,1)S(1)}, u32[]{:S(2)}, u32[]{:S(2)}) %collective-permute-start.1) | collective-permute-done | bytes 65568 | tf_op jit(solution)/shard_map/ppermute | solution.py:266
  16.3 6.0 %collective-permute-start.4 = (bf16[128,256]{1,0:T(8,128)(2,1)S(1)}, bf16[128,256]{1,0:T(8,128)(2,1)S(1)}, u32[]{:S(2)}, u32[]{:S(2)}) collective-permute-start(bf16[128,256]{1,0:T(8,128)(2,1)S(1)} %add.19.refs_0_), channel_id=1, source_target_pairs={{0,10},{1,11},{2,8},{3,9},{4,14},{5,15},{6,12},{7,13},{8,2},{9,3},... | collective-permute-start | bytes 196616 | tf_op jit(solution)/shard_map/ppermute | solution.py:266
  24.0 2.7 %collective-permute-done.3.refs_2_ = bf16[128,256]{1,0:T(8,128)(2,1)S(1)} collective-permute-done((bf16[128,256]{1,0:T(8,128)(2,1)S(1)}, bf16[128,256]{1,0:T(8,128)(2,1)S(1)}, u32[]{:S(2)}, u32[]{:S(2)}) %collective-permute-start.3) | collective-permute-done | bytes 65568 | tf_op jit(solution)/shard_map/ppermute | solution.py:266
  27.7 3.9 %all-gather = bf16[256,256]{1,0:T(8,128)(2,1)S(1)} all-gather(bf16[128,256]{1,0:T(8,128)(2,1)S(1)} %add.20), channel_id=2, replica_groups={{0,1},{2,3},{4,5},{6,7},{8,9},{10,11},{12,13},{14,15},{16,17},{18,19},{..., dimensions={0}, use_global_device_ids=true | all-gather | bytes 196608 | tf_op jit(solution)/shard_map/all_gather | solution.py:286
  31.6 2.6 %first_step.2 = (f32[256,256]{1,0:T(8,128)S(1)}, bf16[128,256]{1,0:T(8,128)(2,1)S(1)}, bf16[128,256]{1,0:T(8,128)(2,1)S(1)}, f32[256,256]{1,0:T(8,128)S(1)}) custom-call(s32[1,2]{1,0:T(1,128)S(1)} %copy-done.4, f32[256,256]{1,0:T(8,128)S(1)} %get-tuple-element.29.vector, f32[256,256]{1,0:T(8,128)S(1)} %get-tuple-element.30.applied, ...), custom_call_target="tpu_custom_call" | custom-call | flops 1677721600 | bytes 6553600 | tf_op jit(solution)/shard_map/first_step/pallas_call | solution.py:263
  35.6 2.2 %collective-permute-start.6 = (bf16[128,256]{1,0:T(8,128)(2,1)S(1)}, bf16[128,256]{1,0:T(8,128)(2,1)S(1)}, u32[]{:S(2)}, u32[]{:S(2)}) collective-permute-start(bf16[128,256]{1,0:T(8,128)(2,1)S(1)} %add.21.refs_0_), channel_id=1, source_target_pairs={{0,2},{1,3},{2,0},{3,1},{4,6},{5,7},{6,4},{7,5},{8,10},{9,11},{10,... | collective-permute-start | bytes 196616 | tf_op jit(solution)/shard_map/ppermute | solution.py:266
  37.8 2.2 %collective-permute-done.6.refs_1_ = bf16[128,256]{1,0:T(8,128)(2,1)S(1)} collective-permute-done((bf16[128,256]{1,0:T(8,128)(2,1)S(1)}, bf16[128,256]{1,0:T(8,128)(2,1)S(1)}, u32[]{:S(2)}, u32[]{:S(2)}) %collective-permute-start.6) | collective-permute-done | bytes 65568 | tf_op jit(solution)/shard_map/ppermute | solution.py:266
  40.0 2.4 %collective-permute-start.9 = (bf16[128,256]{1,0:T(8,128)(2,1)S(1)}, bf16[128,256]{1,0:T(8,128)(2,1)S(1)}, u32[]{:S(2)}, u32[]{:S(2)}) collective-permute-start(bf16[128,256]{1,0:T(8,128)(2,1)S(1)} %add.22.refs_0_), channel_id=1, source_target_pairs={{0,10},{1,11},{2,8},{3,9},{4,14},{5,15},{6,12},{7,13},{8,2},{9,3},... | collective-permute-start | bytes 196616 | tf_op jit(solution)/shard_map/ppermute | solution.py:266
  48.9 4.2 %all-gather.1 = bf16[256,256]{1,0:T(8,128)(2,1)S(1)} all-gather(bf16[128,256]{1,0:T(8,128)(2,1)S(1)} %add.23), channel_id=3, replica_groups={{0,1},{2,3},{4,5},{6,7},{8,9},{10,11},{12,13},{14,15},{16,17},{18,19},{..., dimensions={0}, use_global_device_ids=true | all-gather | bytes 196608 | tf_op jit(solution)/shard_map/all_gather | solution.py:286
  53.1 2.6 %first_step.3 = (f32[256,256]{1,0:T(8,128)S(1)}, bf16[128,256]{1,0:T(8,128)(2,1)S(1)}, bf16[128,256]{1,0:T(8,128)(2,1)S(1)}) custom-call(s32[1,2]{1,0:T(1,128)S(1)} %copy-done.4, f32[256,256]{1,0:T(8,128)S(1)} %get-tuple-element.33.vector, f32[256,256]{1,0:T(8,128)S(1)} %get-tuple-element.34.applied, bf16[2,128,256]{2,1,0:T(8,128)(2,1)S(1)} %bitcast.10, ...), custom_call_target="tpu_custom_call" | custom-call | flops 1677721600 | bytes 6553600 | tf_op jit(solution)/shard_map/first_step/pallas_call | solution.py:263
  58.1 2.1 %collective-permute-done.11.refs_1_ = bf16[128,256]{1,0:T(8,128)(2,1)S(1)} collective-permute-done((bf16[128,256]{1,0:T(8,128)(2,1)S(1)}, bf16[128,256]{1,0:T(8,128)(2,1)S(1)}, u32[]{:S(2)}, u32[]{:S(2)}) %collective-permute-start.11) | collective-permute-done | bytes 65568 | tf_op jit(solution)/shard_map/ppermute | solution.py:266
  60.3 2.5 %collective-permute-start.14 = (bf16[128,256]{1,0:T(8,128)(2,1)S(1)}, bf16[128,256]{1,0:T(8,128)(2,1)S(1)}, u32[]{:S(2)}, u32[]{:S(2)}) collective-permute-start(bf16[128,256]{1,0:T(8,128)(2,1)S(1)} %add.25.refs_0_), channel_id=1, source_target_pairs={{0,10},{1,11},{2,8},{3,9},{4,14},{5,15},{6,12},{7,13},{8,2},{9,3},... | collective-permute-start | bytes 196616 | tf_op jit(solution)/shard_map/ppermute | solution.py:266
  67.4 2.2 %collective-permute-done.12.refs_1_ = bf16[128,256]{1,0:T(8,128)(2,1)S(1)} collective-permute-done((bf16[128,256]{1,0:T(8,128)(2,1)S(1)}, bf16[128,256]{1,0:T(8,128)(2,1)S(1)}, u32[]{:S(2)}, u32[]{:S(2)}) %collective-permute-start.12) | collective-permute-done | bytes 65568 | tf_op jit(solution)/shard_map/ppermute | solution.py:266
  69.7 3.4 %all-gather.2 = bf16[256,256]{1,0:T(8,128)(2,1)S(1)} all-gather(bf16[128,256]{1,0:T(8,128)(2,1)S(1)} %add.26), channel_id=4, replica_groups={{0,1},{2,3},{4,5},{6,7},{8,9},{10,11},{12,13},{14,15},{16,17},{18,19},{..., dimensions={0}, use_global_device_ids=true | all-gather | bytes 196608 | tf_op jit(solution)/shard_map/all_gather | solution.py:286
  73.2 3.4 %second_start.1 = (f32[1,16,256]{2,1,0:T(8,128)}, bf16[256,256]{1,0:T(8,128)(2,1)S(1)}, bf16[128,256]{1,0:T(8,128)(2,1)S(1)}, bf16[128,256]{1,0:T(8,128)(2,1)S(1)}, f32[256,256]{1,0:T(8,128)S(1)}) custom-call(s32[1,2]{1,0:T(1,128)S(1)} %copy-done.4, f32[256,256]{1,0:T(8,128)S(1)} %get-tuple-element.37.vector, bf16[2,128,256]{2,1,0:T(8,128)(2,1)S(1)} %bitcast.7, ...), custom_call_target="tpu_custom_call" | custom-call | flops 1677721600 | bytes 6553600 | tf_op jit(solution)/shard_map/second_start/pallas_call | solution.py:323
  79.1 2.1 %collective-permute-done.17.refs_1_ = bf16[128,256]{1,0:T(8,128)(2,1)S(1)} collective-permute-done((bf16[128,256]{1,0:T(8,128)(2,1)S(1)}, bf16[128,256]{1,0:T(8,128)(2,1)S(1)}, u32[]{:S(2)}, u32[]{:S(2)}) %collective-permute-start.17) | collective-permute-done | bytes 65568 | tf_op jit(solution)/shard_map/ppermute | solution.py:266
  81.2 2.6 %collective-permute-start.20 = (bf16[128,256]{1,0:T(8,128)(2,1)S(1)}, bf16[128,256]{1,0:T(8,128)(2,1)S(1)}, u32[]{:S(2)}, u32[]{:S(2)}) collective-permute-start(bf16[128,256]{1,0:T(8,128)(2,1)S(1)} %add.28.refs_0_), channel_id=1, source_target_pairs={{0,10},{1,11},{2,8},{3,9},{4,14},{5,15},{6,12},{7,13},{8,2},{9,3},... | collective-permute-start | bytes 196616 | tf_op jit(solution)/shard_map/ppermute | solution.py:266
  88.3 2.4 %collective-permute-done.18.refs_1_ = bf16[128,256]{1,0:T(8,128)(2,1)S(1)} collective-permute-done((bf16[128,256]{1,0:T(8,128)(2,1)S(1)}, bf16[128,256]{1,0:T(8,128)(2,1)S(1)}, u32[]{:S(2)}, u32[]{:S(2)}) %collective-permute-start.18) | collective-permute-done | bytes 65568 | tf_op jit(solution)/shard_map/ppermute | solution.py:266
  90.7 3.4 %all-gather.3 = bf16[256,256]{1,0:T(8,128)(2,1)S(1)} all-gather(bf16[128,256]{1,0:T(8,128)(2,1)S(1)} %add.29), channel_id=5, replica_groups={{0,1},{2,3},{4,5},{6,7},{8,9},{10,11},{12,13},{14,15},{16,17},{18,19},{..., dimensions={0}, use_global_device_ids=true | all-gather | bytes 196608 | tf_op jit(solution)/shard_map/all_gather | solution.py:286
  94.1 3.3 %second_step.2 = (f32[256,256]{1,0:T(8,128)S(1)}, bf16[128,256]{1,0:T(8,128)(2,1)S(1)}, bf16[128,256]{1,0:T(8,128)(2,1)S(1)}, f32[256,256]{1,0:T(8,128)S(1)}) custom-call(s32[1,2]{1,0:T(1,128)S(1)} %copy-done.4, f32[256,256]{1,0:T(8,128)S(1)} %get-tuple-element.44.vector, f32[256,256]{1,0:T(8,128)S(1)} %get-tuple-element.45.applied, ...), custom_call_target="tpu_custom_call" | custom-call | flops 1677721600 | bytes 6553600 | tf_op jit(solution)/shard_map/second_step/pallas_call | solution.py:263
  99.9 2.0 %collective-permute-done.22.refs_1_ = bf16[128,256]{1,0:T(8,128)(2,1)S(1)} collective-permute-done((bf16[128,256]{1,0:T(8,128)(2,1)S(1)}, bf16[128,256]{1,0:T(8,128)(2,1)S(1)}, u32[]{:S(2)}, u32[]{:S(2)}) %collective-permute-start.22) | collective-permute-done | bytes 65568 | tf_op jit(solution)/shard_map/ppermute | solution.py:266
  102.0 2.6 %collective-permute-start.25 = (bf16[128,256]{1,0:T(8,128)(2,1)S(1)}, bf16[128,256]{1,0:T(8,128)(2,1)S(1)}, u32[]{:S(2)}, u32[]{:S(2)}) collective-permute-start(bf16[128,256]{1,0:T(8,128)(2,1)S(1)} %add.31.refs_0_), channel_id=1, source_target_pairs={{0,10},{1,11},{2,8},{3,9},{4,14},{5,15},{6,12},{7,13},{8,2},{9,3},... | collective-permute-start | bytes 196616 | tf_op jit(solution)/shard_map/ppermute | solution.py:266
  109.1 2.3 %collective-permute-done.23.refs_1_ = bf16[128,256]{1,0:T(8,128)(2,1)S(1)} collective-permute-done((bf16[128,256]{1,0:T(8,128)(2,1)S(1)}, bf16[128,256]{1,0:T(8,128)(2,1)S(1)}, u32[]{:S(2)}, u32[]{:S(2)}) %collective-permute-start.23) | collective-permute-done | bytes 65568 | tf_op jit(solution)/shard_map/ppermute | solution.py:266
  111.5 3.4 %all-gather.4 = bf16[256,256]{1,0:T(8,128)(2,1)S(1)} all-gather(bf16[128,256]{1,0:T(8,128)(2,1)S(1)} %add.32), channel_id=6, replica_groups={{0,1},{2,3},{4,5},{6,7},{8,9},{10,11},{12,13},{14,15},{16,17},{18,19},{..., dimensions={0}, use_global_device_ids=true | all-gather | bytes 196608 | tf_op jit(solution)/shard_map/all_gather | solution.py:286
  114.9 3.3 %second_step.3 = (f32[256,256]{1,0:T(8,128)S(1)}, bf16[128,256]{1,0:T(8,128)(2,1)S(1)}, bf16[128,256]{1,0:T(8,128)(2,1)S(1)}) custom-call(s32[1,2]{1,0:T(1,128)S(1)} %copy-done.4, f32[256,256]{1,0:T(8,128)S(1)} %get-tuple-element.49.vector, f32[256,256]{1,0:T(8,128)S(1)} %get-tuple-element.50.applied, bf16[2,128,256]{2,1,0:T(8,128)(2,1)S(1)} %bitcast.6, ...), custom_call_target="tpu_custom_call" | custom-call | flops 1677721600 | bytes 6553600 | tf_op jit(solution)/shard_map/second_step/pallas_call | solution.py:263
  120.7 2.0 %collective-permute-done.27.refs_1_ = bf16[128,256]{1,0:T(8,128)(2,1)S(1)} collective-permute-done((bf16[128,256]{1,0:T(8,128)(2,1)S(1)}, bf16[128,256]{1,0:T(8,128)(2,1)S(1)}, u32[]{:S(2)}, u32[]{:S(2)}) %collective-permute-start.27) | collective-permute-done | bytes 65568 | tf_op jit(solution)/shard_map/ppermute | solution.py:266
  122.8 2.6 %collective-permute-start.30 = (bf16[128,256]{1,0:T(8,128)(2,1)S(1)}, bf16[128,256]{1,0:T(8,128)(2,1)S(1)}, u32[]{:S(2)}, u32[]{:S(2)}) collective-permute-start(bf16[128,256]{1,0:T(8,128)(2,1)S(1)} %add.34.refs_0_), channel_id=1, source_target_pairs={{0,10},{1,11},{2,8},{3,9},{4,14},{5,15},{6,12},{7,13},{8,2},{9,3},... | collective-permute-start | bytes 196616 | tf_op jit(solution)/shard_map/ppermute | solution.py:266
  129.9 2.3 %collective-permute-done.28.refs_1_ = bf16[128,256]{1,0:T(8,128)(2,1)S(1)} collective-permute-done((bf16[128,256]{1,0:T(8,128)(2,1)S(1)}, bf16[128,256]{1,0:T(8,128)(2,1)S(1)}, u32[]{:S(2)}, u32[]{:S(2)}) %collective-permute-start.28) | collective-permute-done | bytes 65568 | tf_op jit(solution)/shard_map/ppermute | solution.py:266
  132.3 3.4 %all-gather.5 = bf16[256,256]{1,0:T(8,128)(2,1)S(1)} all-gather(bf16[128,256]{1,0:T(8,128)(2,1)S(1)} %add.35), channel_id=7, replica_groups={{0,1},{2,3},{4,5},{6,7},{8,9},{10,11},{12,13},{14,15},{16,17},{18,19},{..., dimensions={0}, use_global_device_ids=true | all-gather | bytes 196608 | tf_op jit(solution)/shard_map/all_gather | solution.py:286
  (78 shorter events, 45.4 us)
Async XLA Ops:
  3.8 61.3 %collective-permute-start.15 = (bf16[3776,256]{1,0:T(8,128)(2,1)S(1)}, bf16[3776,256]{1,0:T(8,128)(2,1)S(1)}, u32[]{:S(2)}, u32[]{:S(2)}) collective-permute-start(bf16[3776,256]{1,0:T(8,128)(2,1)S(1)} %pack.1), channel_id=1, source_target_pairs={{0,16},{16,32},{32,48},{48,64},{64,80},{80,96},{96,112},{112,128},... | collective-permute-start | bytes 5799944 | tf_op jit(solution)/shard_map/ppermute | solution.py:303
  10.5 1.9 %collective-permute-start = (bf16[128,256]{1,0:T(8,128)(2,1)S(1)}, bf16[128,256]{1,0:T(8,128)(2,1)S(1)}, u32[]{:S(2)}, u32[]{:S(2)}) collective-permute-start(bf16[128,256]{1,0:T(8,128)(2,1)S(1)} %get-tuple-element.32), channel_id=1, source_target_pairs={{0,1},{1,0},{2,3},{3,2},{4,5},{5,4},{6,7},{7,6},{8,9},{9,8},{10,11... | collective-permute-start | bytes 196616 | tf_op jit(solution)/shard_map/ppermute | solution.py:266
  12.5 3.8 %collective-permute-start.1 = (bf16[128,256]{1,0:T(8,128)(2,1)S(1)}, bf16[128,256]{1,0:T(8,128)(2,1)S(1)}, u32[]{:S(2)}, u32[]{:S(2)}) collective-permute-start(bf16[128,256]{1,0:T(8,128)(2,1)S(1)} %add.18.refs_0_), channel_id=1, source_target_pairs={{0,2},{1,3},{2,0},{3,1},{4,6},{5,7},{6,4},{7,5},{8,10},{9,11},{10,... | collective-permute-start | bytes 196616 | tf_op jit(solution)/shard_map/ppermute | solution.py:266
  16.3 7.7 %collective-permute-start.4 = (bf16[128,256]{1,0:T(8,128)(2,1)S(1)}, bf16[128,256]{1,0:T(8,128)(2,1)S(1)}, u32[]{:S(2)}, u32[]{:S(2)}) collective-permute-start(bf16[128,256]{1,0:T(8,128)(2,1)S(1)} %add.19.refs_0_), channel_id=1, source_target_pairs={{0,10},{1,11},{2,8},{3,9},{4,14},{5,15},{6,12},{7,13},{8,2},{9,3},... | collective-permute-start | bytes 196616 | tf_op jit(solution)/shard_map/ppermute | solution.py:266
  22.2 4.5 %collective-permute-start.3 = (bf16[128,256]{1,0:T(8,128)(2,1)S(1)}, bf16[128,256]{1,0:T(8,128)(2,1)S(1)}, u32[]{:S(2)}, u32[]{:S(2)}) collective-permute-start(bf16[128,256]{1,0:T(8,128)(2,1)S(1)} %add.19.refs_0_), channel_id=1, source_target_pairs={{0,14},{1,15},{2,4},{3,5},{4,2},{5,3},{6,8},{7,9},{8,6},{9,7},{10,... | collective-permute-start | bytes 196616 | tf_op jit(solution)/shard_map/ppermute | solution.py:266
  22.3 5.4 %collective-permute-start.2 = (bf16[128,256]{1,0:T(8,128)(2,1)S(1)}, bf16[128,256]{1,0:T(8,128)(2,1)S(1)}, u32[]{:S(2)}, u32[]{:S(2)}) collective-permute-start(bf16[128,256]{1,0:T(8,128)(2,1)S(1)} %add.19.refs_0_), channel_id=1, source_target_pairs={{0,12},{1,13},{2,6},{3,7},{4,0},{5,1},{6,10},{7,11},{8,4},{9,5},{1... | collective-permute-start | bytes 196616 | tf_op jit(solution)/shard_map/ppermute | solution.py:266
  34.2 1.3 collective-permute-start.5
  35.6 4.4 %collective-permute-start.6 = (bf16[128,256]{1,0:T(8,128)(2,1)S(1)}, bf16[128,256]{1,0:T(8,128)(2,1)S(1)}, u32[]{:S(2)}, u32[]{:S(2)}) collective-permute-start(bf16[128,256]{1,0:T(8,128)(2,1)S(1)} %add.21.refs_0_), channel_id=1, source_target_pairs={{0,2},{1,3},{2,0},{3,1},{4,6},{5,7},{6,4},{7,5},{8,10},{9,11},{10,... | collective-permute-start | bytes 196616 | tf_op jit(solution)/shard_map/ppermute | solution.py:266
  40.0 6.2 %collective-permute-start.9 = (bf16[128,256]{1,0:T(8,128)(2,1)S(1)}, bf16[128,256]{1,0:T(8,128)(2,1)S(1)}, u32[]{:S(2)}, u32[]{:S(2)}) collective-permute-start(bf16[128,256]{1,0:T(8,128)(2,1)S(1)} %add.22.refs_0_), channel_id=1, source_target_pairs={{0,10},{1,11},{2,8},{3,9},{4,14},{5,15},{6,12},{7,13},{8,2},{9,3},... | collective-permute-start | bytes 196616 | tf_op jit(solution)/shard_map/ppermute | solution.py:266
  42.4 5.3 %collective-permute-start.8 = (bf16[128,256]{1,0:T(8,128)(2,1)S(1)}, bf16[128,256]{1,0:T(8,128)(2,1)S(1)}, u32[]{:S(2)}, u32[]{:S(2)}) collective-permute-start(bf16[128,256]{1,0:T(8,128)(2,1)S(1)} %add.22.refs_0_), channel_id=1, source_target_pairs={{0,14},{1,15},{2,4},{3,5},{4,2},{5,3},{6,8},{7,9},{8,6},{9,7},{10,... | collective-permute-start | bytes 196616 | tf_op jit(solution)/shard_map/ppermute | solution.py:266
  43.9 5.0 %collective-permute-start.7 = (bf16[128,256]{1,0:T(8,128)(2,1)S(1)}, bf16[128,256]{1,0:T(8,128)(2,1)S(1)}, u32[]{:S(2)}, u32[]{:S(2)}) collective-permute-start(bf16[128,256]{1,0:T(8,128)(2,1)S(1)} %add.22.refs_0_), channel_id=1, source_target_pairs={{0,12},{1,13},{2,6},{3,7},{4,0},{5,1},{6,10},{7,11},{8,4},{9,5},{1... | collective-permute-start | bytes 196616 | tf_op jit(solution)/shard_map/ppermute | solution.py:266
  53.1 12.0 %copy-start.3 = (bf16[1,256,256]{2,1,0:T(8,128)(2,1)S(1)}, bf16[1,256,256]{2,1,0:T(8,128)(2,1)}, u32[]{:S(2)}) copy-start(bf16[1,256,256]{2,1,0:T(8,128)(2,1)} %start.3) | copy-start | bytes 393220
  55.7 1.3 collective-permute-start.10
  57.1 3.2 %collective-permute-start.11 = (bf16[128,256]{1,0:T(8,128)(2,1)S(1)}, bf16[128,256]{1,0:T(8,128)(2,1)S(1)}, u32[]{:S(2)}, u32[]{:S(2)}) collective-permute-start(bf16[128,256]{1,0:T(8,128)(2,1)S(1)} %add.24.refs_0_), channel_id=1, source_target_pairs={{0,2},{1,3},{2,0},{3,1},{4,6},{5,7},{6,4},{7,5},{8,10},{9,11},{10,... | collective-permute-start | bytes 196616 | tf_op jit(solution)/shard_map/ppermute | solution.py:266
  60.3 6.4 %collective-permute-start.14 = (bf16[128,256]{1,0:T(8,128)(2,1)S(1)}, bf16[128,256]{1,0:T(8,128)(2,1)S(1)}, u32[]{:S(2)}, u32[]{:S(2)}) collective-permute-start(bf16[128,256]{1,0:T(8,128)(2,1)S(1)} %add.25.refs_0_), channel_id=1, source_target_pairs={{0,10},{1,11},{2,8},{3,9},{4,14},{5,15},{6,12},{7,13},{8,2},{9,3},... | collective-permute-start | bytes 196616 | tf_op jit(solution)/shard_map/ppermute | solution.py:266
  62.8 4.6 %collective-permute-start.13 = (bf16[128,256]{1,0:T(8,128)(2,1)S(1)}, bf16[128,256]{1,0:T(8,128)(2,1)S(1)}, u32[]{:S(2)}, u32[]{:S(2)}) collective-permute-start(bf16[128,256]{1,0:T(8,128)(2,1)S(1)} %add.25.refs_0_), channel_id=1, source_target_pairs={{0,14},{1,15},{2,4},{3,5},{4,2},{5,3},{6,8},{7,9},{8,6},{9,7},{10,... | collective-permute-start | bytes 196616 | tf_op jit(solution)/shard_map/ppermute | solution.py:266
  64.2 5.5 %collective-permute-start.12 = (bf16[128,256]{1,0:T(8,128)(2,1)S(1)}, bf16[128,256]{1,0:T(8,128)(2,1)S(1)}, u32[]{:S(2)}, u32[]{:S(2)}) collective-permute-start(bf16[128,256]{1,0:T(8,128)(2,1)S(1)} %add.25.refs_0_), channel_id=1, source_target_pairs={{0,12},{1,13},{2,6},{3,7},{4,0},{5,1},{6,10},{7,11},{8,4},{9,5},{1... | collective-permute-start | bytes 196616 | tf_op jit(solution)/shard_map/ppermute | solution.py:266
  76.6 1.3 collective-permute-start.16
  78.0 3.2 %collective-permute-start.17 = (bf16[128,256]{1,0:T(8,128)(2,1)S(1)}, bf16[128,256]{1,0:T(8,128)(2,1)S(1)}, u32[]{:S(2)}, u32[]{:S(2)}) collective-permute-start(bf16[128,256]{1,0:T(8,128)(2,1)S(1)} %add.27.refs_0_), channel_id=1, source_target_pairs={{0,2},{1,3},{2,0},{3,1},{4,6},{5,7},{6,4},{7,5},{8,10},{9,11},{10,... | collective-permute-start | bytes 196616 | tf_op jit(solution)/shard_map/ppermute | solution.py:266
  81.2 6.3 %collective-permute-start.20 = (bf16[128,256]{1,0:T(8,128)(2,1)S(1)}, bf16[128,256]{1,0:T(8,128)(2,1)S(1)}, u32[]{:S(2)}, u32[]{:S(2)}) collective-permute-start(bf16[128,256]{1,0:T(8,128)(2,1)S(1)} %add.28.refs_0_), channel_id=1, source_target_pairs={{0,10},{1,11},{2,8},{3,9},{4,14},{5,15},{6,12},{7,13},{8,2},{9,3},... | collective-permute-start | bytes 196616 | tf_op jit(solution)/shard_map/ppermute | solution.py:266
  83.8 4.5 %collective-permute-start.19 = (bf16[128,256]{1,0:T(8,128)(2,1)S(1)}, bf16[128,256]{1,0:T(8,128)(2,1)S(1)}, u32[]{:S(2)}, u32[]{:S(2)}) collective-permute-start(bf16[128,256]{1,0:T(8,128)(2,1)S(1)} %add.28.refs_0_), channel_id=1, source_target_pairs={{0,14},{1,15},{2,4},{3,5},{4,2},{5,3},{6,8},{7,9},{8,6},{9,7},{10,... | collective-permute-start | bytes 196616 | tf_op jit(solution)/shard_map/ppermute | solution.py:266
  85.2 5.5 %collective-permute-start.18 = (bf16[128,256]{1,0:T(8,128)(2,1)S(1)}, bf16[128,256]{1,0:T(8,128)(2,1)S(1)}, u32[]{:S(2)}, u32[]{:S(2)}) collective-permute-start(bf16[128,256]{1,0:T(8,128)(2,1)S(1)} %add.28.refs_0_), channel_id=1, source_target_pairs={{0,12},{1,13},{2,6},{3,7},{4,0},{5,1},{6,10},{7,11},{8,4},{9,5},{1... | collective-permute-start | bytes 196616 | tf_op jit(solution)/shard_map/ppermute | solution.py:266
  97.4 1.3 collective-permute-start.21
  98.7 3.2 %collective-permute-start.22 = (bf16[128,256]{1,0:T(8,128)(2,1)S(1)}, bf16[128,256]{1,0:T(8,128)(2,1)S(1)}, u32[]{:S(2)}, u32[]{:S(2)}) collective-permute-start(bf16[128,256]{1,0:T(8,128)(2,1)S(1)} %add.30.refs_0_), channel_id=1, source_target_pairs={{0,2},{1,3},{2,0},{3,1},{4,6},{5,7},{6,4},{7,5},{8,10},{9,11},{10,... | collective-permute-start | bytes 196616 | tf_op jit(solution)/shard_map/ppermute | solution.py:266
  102.0 6.3 %collective-permute-start.25 = (bf16[128,256]{1,0:T(8,128)(2,1)S(1)}, bf16[128,256]{1,0:T(8,128)(2,1)S(1)}, u32[]{:S(2)}, u32[]{:S(2)}) collective-permute-start(bf16[128,256]{1,0:T(8,128)(2,1)S(1)} %add.31.refs_0_), channel_id=1, source_target_pairs={{0,10},{1,11},{2,8},{3,9},{4,14},{5,15},{6,12},{7,13},{8,2},{9,3},... | collective-permute-start | bytes 196616 | tf_op jit(solution)/shard_map/ppermute | solution.py:266
  104.6 4.5 %collective-permute-start.24 = (bf16[128,256]{1,0:T(8,128)(2,1)S(1)}, bf16[128,256]{1,0:T(8,128)(2,1)S(1)}, u32[]{:S(2)}, u32[]{:S(2)}) collective-permute-start(bf16[128,256]{1,0:T(8,128)(2,1)S(1)} %add.31.refs_0_), channel_id=1, source_target_pairs={{0,14},{1,15},{2,4},{3,5},{4,2},{5,3},{6,8},{7,9},{8,6},{9,7},{10,... | collective-permute-start | bytes 196616 | tf_op jit(solution)/shard_map/ppermute | solution.py:266
  106.0 5.5 %collective-permute-start.23 = (bf16[128,256]{1,0:T(8,128)(2,1)S(1)}, bf16[128,256]{1,0:T(8,128)(2,1)S(1)}, u32[]{:S(2)}, u32[]{:S(2)}) collective-permute-start(bf16[128,256]{1,0:T(8,128)(2,1)S(1)} %add.31.refs_0_), channel_id=1, source_target_pairs={{0,12},{1,13},{2,6},{3,7},{4,0},{5,1},{6,10},{7,11},{8,4},{9,5},{1... | collective-permute-start | bytes 196616 | tf_op jit(solution)/shard_map/ppermute | solution.py:266
  118.2 1.3 collective-permute-start.26
  119.6 3.2 %collective-permute-start.27 = (bf16[128,256]{1,0:T(8,128)(2,1)S(1)}, bf16[128,256]{1,0:T(8,128)(2,1)S(1)}, u32[]{:S(2)}, u32[]{:S(2)}) collective-permute-start(bf16[128,256]{1,0:T(8,128)(2,1)S(1)} %add.33.refs_0_), channel_id=1, source_target_pairs={{0,2},{1,3},{2,0},{3,1},{4,6},{5,7},{6,4},{7,5},{8,10},{9,11},{10,... | collective-permute-start | bytes 196616 | tf_op jit(solution)/shard_map/ppermute | solution.py:266
  122.8 6.3 %collective-permute-start.30 = (bf16[128,256]{1,0:T(8,128)(2,1)S(1)}, bf16[128,256]{1,0:T(8,128)(2,1)S(1)}, u32[]{:S(2)}, u32[]{:S(2)}) collective-permute-start(bf16[128,256]{1,0:T(8,128)(2,1)S(1)} %add.34.refs_0_), channel_id=1, source_target_pairs={{0,10},{1,11},{2,8},{3,9},{4,14},{5,15},{6,12},{7,13},{8,2},{9,3},... | collective-permute-start | bytes 196616 | tf_op jit(solution)/shard_map/ppermute | solution.py:266
  125.4 4.5 %collective-permute-start.29 = (bf16[128,256]{1,0:T(8,128)(2,1)S(1)}, bf16[128,256]{1,0:T(8,128)(2,1)S(1)}, u32[]{:S(2)}, u32[]{:S(2)}) collective-permute-start(bf16[128,256]{1,0:T(8,128)(2,1)S(1)} %add.34.refs_0_), channel_id=1, source_target_pairs={{0,14},{1,15},{2,4},{3,5},{4,2},{5,3},{6,8},{7,9},{8,6},{9,7},{10,... | collective-permute-start | bytes 196616 | tf_op jit(solution)/shard_map/ppermute | solution.py:266
  126.8 5.5 %collective-permute-start.28 = (bf16[128,256]{1,0:T(8,128)(2,1)S(1)}, bf16[128,256]{1,0:T(8,128)(2,1)S(1)}, u32[]{:S(2)}, u32[]{:S(2)}) collective-permute-start(bf16[128,256]{1,0:T(8,128)(2,1)S(1)} %add.34.refs_0_), channel_id=1, source_target_pairs={{0,12},{1,13},{2,6},{3,7},{4,0},{5,1},{6,10},{7,11},{8,4},{9,5},{1... | collective-permute-start | bytes 196616 | tf_op jit(solution)/shard_map/ppermute | solution.py:266
  (6 other events, 21.7 us)

commit v3 on v2

--- a/solution.py
+++ b/solution.py
@@ -81,11 +81,12 @@
             acc[...] += total
 
 
-def hand_out(acc, mine, theirs):
+def hand_out(found, mine, theirs):
     half = mine.shape[0]
-    core = lax.rem(lax.axis_index("sec"), 2)
-    mine[...] = acc[pl.ds(pl.multiple_of(core * half, half), half), :].astype(BF16)
-    theirs[...] = acc[pl.ds(pl.multiple_of((1 - core) * half, half), half), :].astype(BF16)
+    low = lax.rem(lax.axis_index("sec"), 2) == 0
+    upper, lower = found[:half], found[half:]
+    mine[...] = jnp.where(low, upper, lower).astype(BF16)
+    theirs[...] = jnp.where(low, lower, upper).astype(BF16)
 
 
 def first_start(kept, start, left, right, vector, mine, theirs, applied, acc):
@@ -94,8 +95,9 @@
     scale = states / jnp.sqrt(jnp.sum(block * block) + EPSILON)
     vector[...] = block * scale
     contract(block.astype(BF16), left.at[0], right.at[0], acc)
-    applied[...] = acc[...] * scale
-    hand_out(applied, mine, theirs)
+    found = acc[...] * scale
+    applied[...] = found
+    hand_out(found, mine, theirs)
 
 
 def first_step(
@@ -105,8 +107,9 @@
     a, b = coefficients(current, product)
     contract(product.astype(BF16), left.at[0], right.at[0], acc)
     after[...] = a * current + b * product
-    applied_after[...] = a * applied[...] + b * acc[...]
-    hand_out(applied_after, mine, theirs)
+    found = a * applied[...] + b * acc[...]
+    applied_after[...] = found
+    hand_out(found, mine, theirs)
 
 
 def place(shape):
@@ -182,13 +185,17 @@
     kept, vector, summed, turned, edge, incoming, right, rows, site, mine, theirs, applied, acc
 ):
     states = vector.shape[1]
-    acc[...] = stepped(vector, summed, kept[0, 0])
+    current, product = vector[...], joined(summed, kept[0, 0])
+    a, b = coefficients(current, product)
+    old, new = dot(turned[...], current.astype(BF16)), dot(turned[...], product.astype(BF16))
+    acc[...] = a * current + b * product
     own_rows(acc, rows)
     site_left = (acc[...] * states**-0.5).astype(BF16)
     site[...] = site_left
-    inner = dot(turned[...], site_left).astype(BF16)
-    applied[...] = second_apply(inner, edge, site_left, incoming, right, acc)
-    hand_out(applied, mine, theirs)
+    inner = ((a * states**-0.5) * old + (b * states**-0.5) * new).astype(BF16)
+    found = second_apply(inner, edge, site_left, incoming, right, acc)
+    applied[...] = found
+    hand_out(found, mine, theirs)
 
 
 def second_step(
@@ -201,8 +208,9 @@
     inner = dot(edge[...], inner).astype(BF16)
     found = second_apply(inner, edge, site[...], incoming, right, acc)
     after[...] = a * current + b * product
-    applied_after[...] = a * applied[...] + b * found
-    hand_out(applied_after, mine, theirs)
+    found = a * applied[...] + b * found
+    applied_after[...] = found
+    hand_out(found, mine, theirs)
 
 
 def second_end(kept, vector, summed, rows):

time: 137 us -> 137 us (level)
  no operation moved by 1% of the time
where the time goes in v3:
time: 137 us
  starting transfers between devices  46.3 us (34%)
  waiting for transfers between devices  43.8 us (32%)
  Pallas kernels  22.4 us (16%)
  blocking collectives  21.8 us (16%)
  local copies, waits for them, and re-layouts  1.92 us (1%)
    ppermute x30, waiting for transfers between devices, moved(): lax.ppermute(value, 'sec', [(n, target(n) % sections) for n in range(sect...  43.8 us
    ppermute x30, starting transfers between devices, moved(): lax.ppermute(value, 'sec', [(n, target(n) % sections) for n in range(sect...  42.2 us
    all_gather x6, blocking collectives, summed(): return (lax.all_gather(total, 'sec', axis=0, axis_index_groups=cores),)  21.8 us
    pallas_call x4, Pallas kernels, step_call(): call(kernel, specs, outs, scratch, cost=apply_cost)  11.6 us
    ppermute x1, starting transfers between devices, on_device(): lax.ppermute(package, 'seg', [(n, n + 1) for n in range(segments - 1)])  4.07 us
    pallas_call x1, Pallas kernels, on_device(): call(second_start, [smem, vmem, tuple((vmem for _ in total)), *[vmem] * 4...  3.54 us
  transfers between devices with their start and end apart: 31, of which 29 were waited for; matrix products, arithmetic and copies ran while one was open for 0% of the time, Pallas kernels for 7%

profile of v3, /device:TPU:1, one launch (start us, length us, event | category | flops | bytes accessed | tf_op | source)
XLA Modules:
  0.0 137.1 jit_solution(8769004514948956538)
XLA Ops:
  0.7 1.9 %copy-done.1 = bf16[1,25,256,256]{3,2,1,0:T(8,128)(2,1)S(1)} copy-done((bf16[1,25,256,256]{3,2,1,0:T(8,128)(2,1)S(1)}, bf16[1,25,256,256]{3,2,1,0:T(8,128)(2,1)}, u32[]{:S(2)}) %copy-start.1) | copy-done | bytes 3276824
  3.8 4.1 %collective-permute-start.15 = (bf16[3776,256]{1,0:T(8,128)(2,1)S(1)}, bf16[3776,256]{1,0:T(8,128)(2,1)S(1)}, u32[]{:S(2)}, u32[]{:S(2)}) collective-permute-start(bf16[3776,256]{1,0:T(8,128)(2,1)S(1)} %pack.1), channel_id=1, source_target_pairs={{0,16},{16,32},{32,48},{48,64},{64,80},{80,96},{96,112},{112,128},... | collective-permute-start | bytes 5799944 | tf_op jit(solution)/shard_map/ppermute | solution.py:311
  7.9 2.5 %first_start.1 = (f32[256,256]{1,0:T(8,128)S(1)}, bf16[128,256]{1,0:T(8,128)(2,1)S(1)}, bf16[128,256]{1,0:T(8,128)(2,1)S(1)}, f32[256,256]{1,0:T(8,128)S(1)}) custom-call(s32[1,2]{1,0:T(1,128)S(1)} %copy-done.4, bf16[1,256,256]{2,1,0:T(8,128)(2,1)S(1)} %copy-done.2, bf16[1,25,256,256]{3,2,1,0:T(8,128)(2,1)S(1)} %copy-done.1, ...), custom_call_target="tpu_custom_call" | custom-call | flops 1677721600 | bytes 6553600 | tf_op jit(solution)/shard_map/first_start/pallas_call | solution.py:313
  14.2 2.1 %collective-permute-done.1.refs_1_ = bf16[128,256]{1,0:T(8,128)(2,1)S(1)} collective-permute-done((bf16[128,256]{1,0:T(8,128)(2,1)S(1)}, bf16[128,256]{1,0:T(8,128)(2,1)S(1)}, u32[]{:S(2)}, u32[]{:S(2)}) %collective-permute-start.1) | collective-permute-done | bytes 65568 | tf_op jit(solution)/shard_map/ppermute | solution.py:274
  16.2 6.0 %collective-permute-start.4 = (bf16[128,256]{1,0:T(8,128)(2,1)S(1)}, bf16[128,256]{1,0:T(8,128)(2,1)S(1)}, u32[]{:S(2)}, u32[]{:S(2)}) collective-permute-start(bf16[128,256]{1,0:T(8,128)(2,1)S(1)} %add.19.refs_0_), channel_id=1, source_target_pairs={{0,10},{1,11},{2,8},{3,9},{4,14},{5,15},{6,12},{7,13},{8,2},{9,3},... | collective-permute-start | bytes 196616 | tf_op jit(solution)/shard_map/ppermute | solution.py:274
  24.0 2.7 %collective-permute-done.3.refs_2_ = bf16[128,256]{1,0:T(8,128)(2,1)S(1)} collective-permute-done((bf16[128,256]{1,0:T(8,128)(2,1)S(1)}, bf16[128,256]{1,0:T(8,128)(2,1)S(1)}, u32[]{:S(2)}, u32[]{:S(2)}) %collective-permute-start.3) | collective-permute-done | bytes 65568 | tf_op jit(solution)/shard_map/ppermute | solution.py:274
  27.6 3.9 %all-gather = bf16[256,256]{1,0:T(8,128)(2,1)S(1)} all-gather(bf16[128,256]{1,0:T(8,128)(2,1)S(1)} %add.20), channel_id=2, replica_groups={{0,1},{2,3},{4,5},{6,7},{8,9},{10,11},{12,13},{14,15},{16,17},{18,19},{..., dimensions={0}, use_global_device_ids=true | all-gather | bytes 196608 | tf_op jit(solution)/shard_map/all_gather | solution.py:294
  31.6 2.6 %first_step.2 = (f32[256,256]{1,0:T(8,128)S(1)}, bf16[128,256]{1,0:T(8,128)(2,1)S(1)}, bf16[128,256]{1,0:T(8,128)(2,1)S(1)}, f32[256,256]{1,0:T(8,128)S(1)}) custom-call(s32[1,2]{1,0:T(1,128)S(1)} %copy-done.4, f32[256,256]{1,0:T(8,128)S(1)} %get-tuple-element.29.vector, f32[256,256]{1,0:T(8,128)S(1)} %get-tuple-element.30.applied, ...), custom_call_target="tpu_custom_call" | custom-call | flops 1677721600 | bytes 6553600 | tf_op jit(solution)/shard_map/first_step/pallas_call | solution.py:271
  35.5 2.2 %collective-permute-start.6 = (bf16[128,256]{1,0:T(8,128)(2,1)S(1)}, bf16[128,256]{1,0:T(8,128)(2,1)S(1)}, u32[]{:S(2)}, u32[]{:S(2)}) collective-permute-start(bf16[128,256]{1,0:T(8,128)(2,1)S(1)} %add.21.refs_0_), channel_id=1, source_target_pairs={{0,2},{1,3},{2,0},{3,1},{4,6},{5,7},{6,4},{7,5},{8,10},{9,11},{10,... | collective-permute-start | bytes 196616 | tf_op jit(solution)/shard_map/ppermute | solution.py:274
  37.7 2.2 %collective-permute-done.6.refs_1_ = bf16[128,256]{1,0:T(8,128)(2,1)S(1)} collective-permute-done((bf16[128,256]{1,0:T(8,128)(2,1)S(1)}, bf16[128,256]{1,0:T(8,128)(2,1)S(1)}, u32[]{:S(2)}, u32[]{:S(2)}) %collective-permute-start.6) | collective-permute-done | bytes 65568 | tf_op jit(solution)/shard_map/ppermute | solution.py:274
  39.9 2.4 %collective-permute-start.9 = (bf16[128,256]{1,0:T(8,128)(2,1)S(1)}, bf16[128,256]{1,0:T(8,128)(2,1)S(1)}, u32[]{:S(2)}, u32[]{:S(2)}) collective-permute-start(bf16[128,256]{1,0:T(8,128)(2,1)S(1)} %add.22.refs_0_), channel_id=1, source_target_pairs={{0,10},{1,11},{2,8},{3,9},{4,14},{5,15},{6,12},{7,13},{8,2},{9,3},... | collective-permute-start | bytes 196616 | tf_op jit(solution)/shard_map/ppermute | solution.py:274
  48.8 4.2 %all-gather.1 = bf16[256,256]{1,0:T(8,128)(2,1)S(1)} all-gather(bf16[128,256]{1,0:T(8,128)(2,1)S(1)} %add.23), channel_id=3, replica_groups={{0,1},{2,3},{4,5},{6,7},{8,9},{10,11},{12,13},{14,15},{16,17},{18,19},{..., dimensions={0}, use_global_device_ids=true | all-gather | bytes 196608 | tf_op jit(solution)/shard_map/all_gather | solution.py:294
  53.0 2.6 %first_step.3 = (f32[256,256]{1,0:T(8,128)S(1)}, bf16[128,256]{1,0:T(8,128)(2,1)S(1)}, bf16[128,256]{1,0:T(8,128)(2,1)S(1)}) custom-call(s32[1,2]{1,0:T(1,128)S(1)} %copy-done.4, f32[256,256]{1,0:T(8,128)S(1)} %get-tuple-element.33.vector, f32[256,256]{1,0:T(8,128)S(1)} %get-tuple-element.34.applied, bf16[2,128,256]{2,1,0:T(8,128)(2,1)S(1)} %bitcast.10, ...), custom_call_target="tpu_custom_call" | custom-call | flops 1677721600 | bytes 6553600 | tf_op jit(solution)/shard_map/first_step/pallas_call | solution.py:271
  58.0 2.1 %collective-permute-done.11.refs_1_ = bf16[128,256]{1,0:T(8,128)(2,1)S(1)} collective-permute-done((bf16[128,256]{1,0:T(8,128)(2,1)S(1)}, bf16[128,256]{1,0:T(8,128)(2,1)S(1)}, u32[]{:S(2)}, u32[]{:S(2)}) %collective-permute-start.11) | collective-permute-done | bytes 65568 | tf_op jit(solution)/shard_map/ppermute | solution.py:274
  60.2 2.5 %collective-permute-start.14 = (bf16[128,256]{1,0:T(8,128)(2,1)S(1)}, bf16[128,256]{1,0:T(8,128)(2,1)S(1)}, u32[]{:S(2)}, u32[]{:S(2)}) collective-permute-start(bf16[128,256]{1,0:T(8,128)(2,1)S(1)} %add.25.refs_0_), channel_id=1, source_target_pairs={{0,10},{1,11},{2,8},{3,9},{4,14},{5,15},{6,12},{7,13},{8,2},{9,3},... | collective-permute-start | bytes 196616 | tf_op jit(solution)/shard_map/ppermute | solution.py:274
  67.3 2.3 %collective-permute-done.12.refs_1_ = bf16[128,256]{1,0:T(8,128)(2,1)S(1)} collective-permute-done((bf16[128,256]{1,0:T(8,128)(2,1)S(1)}, bf16[128,256]{1,0:T(8,128)(2,1)S(1)}, u32[]{:S(2)}, u32[]{:S(2)}) %collective-permute-start.12) | collective-permute-done | bytes 65568 | tf_op jit(solution)/shard_map/ppermute | solution.py:274
  69.6 3.4 %all-gather.2 = bf16[256,256]{1,0:T(8,128)(2,1)S(1)} all-gather(bf16[128,256]{1,0:T(8,128)(2,1)S(1)} %add.26), channel_id=4, replica_groups={{0,1},{2,3},{4,5},{6,7},{8,9},{10,11},{12,13},{14,15},{16,17},{18,19},{..., dimensions={0}, use_global_device_ids=true | all-gather | bytes 196608 | tf_op jit(solution)/shard_map/all_gather | solution.py:294
  73.1 3.5 %second_start.1 = (f32[1,16,256]{2,1,0:T(8,128)}, bf16[256,256]{1,0:T(8,128)(2,1)S(1)}, bf16[128,256]{1,0:T(8,128)(2,1)S(1)}, bf16[128,256]{1,0:T(8,128)(2,1)S(1)}, f32[256,256]{1,0:T(8,128)S(1)}) custom-call(s32[1,2]{1,0:T(1,128)S(1)} %copy-done.4, f32[256,256]{1,0:T(8,128)S(1)} %get-tuple-element.37.vector, bf16[2,128,256]{2,1,0:T(8,128)(2,1)S(1)} %bitcast.7, ...), custom_call_target="tpu_custom_call" | custom-call | flops 1677721600 | bytes 6553600 | tf_op jit(solution)/shard_map/second_start/pallas_call | solution.py:331
  79.0 2.1 %collective-permute-done.17.refs_1_ = bf16[128,256]{1,0:T(8,128)(2,1)S(1)} collective-permute-done((bf16[128,256]{1,0:T(8,128)(2,1)S(1)}, bf16[128,256]{1,0:T(8,128)(2,1)S(1)}, u32[]{:S(2)}, u32[]{:S(2)}) %collective-permute-start.17) | collective-permute-done | bytes 65568 | tf_op jit(solution)/shard_map/ppermute | solution.py:274
  81.1 2.6 %collective-permute-start.20 = (bf16[128,256]{1,0:T(8,128)(2,1)S(1)}, bf16[128,256]{1,0:T(8,128)(2,1)S(1)}, u32[]{:S(2)}, u32[]{:S(2)}) collective-permute-start(bf16[128,256]{1,0:T(8,128)(2,1)S(1)} %add.28.refs_0_), channel_id=1, source_target_pairs={{0,10},{1,11},{2,8},{3,9},{4,14},{5,15},{6,12},{7,13},{8,2},{9,3},... | collective-permute-start | bytes 196616 | tf_op jit(solution)/shard_map/ppermute | solution.py:274
  88.2 2.3 %collective-permute-done.18.refs_1_ = bf16[128,256]{1,0:T(8,128)(2,1)S(1)} collective-permute-done((bf16[128,256]{1,0:T(8,128)(2,1)S(1)}, bf16[128,256]{1,0:T(8,128)(2,1)S(1)}, u32[]{:S(2)}, u32[]{:S(2)}) %collective-permute-start.18) | collective-permute-done | bytes 65568 | tf_op jit(solution)/shard_map/ppermute | solution.py:274
  90.6 3.4 %all-gather.3 = bf16[256,256]{1,0:T(8,128)(2,1)S(1)} all-gather(bf16[128,256]{1,0:T(8,128)(2,1)S(1)} %add.29), channel_id=5, replica_groups={{0,1},{2,3},{4,5},{6,7},{8,9},{10,11},{12,13},{14,15},{16,17},{18,19},{..., dimensions={0}, use_global_device_ids=true | all-gather | bytes 196608 | tf_op jit(solution)/shard_map/all_gather | solution.py:294
  94.0 3.2 %second_step.2 = (f32[256,256]{1,0:T(8,128)S(1)}, bf16[128,256]{1,0:T(8,128)(2,1)S(1)}, bf16[128,256]{1,0:T(8,128)(2,1)S(1)}, f32[256,256]{1,0:T(8,128)S(1)}) custom-call(s32[1,2]{1,0:T(1,128)S(1)} %copy-done.4, f32[256,256]{1,0:T(8,128)S(1)} %get-tuple-element.44.vector, f32[256,256]{1,0:T(8,128)S(1)} %get-tuple-element.45.applied, ...), custom_call_target="tpu_custom_call" | custom-call | flops 1677721600 | bytes 6553600 | tf_op jit(solution)/shard_map/second_step/pallas_call | solution.py:271
  99.8 2.0 %collective-permute-done.22.refs_1_ = bf16[128,256]{1,0:T(8,128)(2,1)S(1)} collective-permute-done((bf16[128,256]{1,0:T(8,128)(2,1)S(1)}, bf16[128,256]{1,0:T(8,128)(2,1)S(1)}, u32[]{:S(2)}, u32[]{:S(2)}) %collective-permute-start.22) | collective-permute-done | bytes 65568 | tf_op jit(solution)/shard_map/ppermute | solution.py:274
  101.9 2.6 %collective-permute-start.25 = (bf16[128,256]{1,0:T(8,128)(2,1)S(1)}, bf16[128,256]{1,0:T(8,128)(2,1)S(1)}, u32[]{:S(2)}, u32[]{:S(2)}) collective-permute-start(bf16[128,256]{1,0:T(8,128)(2,1)S(1)} %add.31.refs_0_), channel_id=1, source_target_pairs={{0,10},{1,11},{2,8},{3,9},{4,14},{5,15},{6,12},{7,13},{8,2},{9,3},... | collective-permute-start | bytes 196616 | tf_op jit(solution)/shard_map/ppermute | solution.py:274
  109.0 2.3 %collective-permute-done.23.refs_1_ = bf16[128,256]{1,0:T(8,128)(2,1)S(1)} collective-permute-done((bf16[128,256]{1,0:T(8,128)(2,1)S(1)}, bf16[128,256]{1,0:T(8,128)(2,1)S(1)}, u32[]{:S(2)}, u32[]{:S(2)}) %collective-permute-start.23) | collective-permute-done | bytes 65568 | tf_op jit(solution)/shard_map/ppermute | solution.py:274
  111.4 3.4 %all-gather.4 = bf16[256,256]{1,0:T(8,128)(2,1)S(1)} all-gather(bf16[128,256]{1,0:T(8,128)(2,1)S(1)} %add.32), channel_id=6, replica_groups={{0,1},{2,3},{4,5},{6,7},{8,9},{10,11},{12,13},{14,15},{16,17},{18,19},{..., dimensions={0}, use_global_device_ids=true | all-gather | bytes 196608 | tf_op jit(solution)/shard_map/all_gather | solution.py:294
  114.8 3.2 %second_step.3 = (f32[256,256]{1,0:T(8,128)S(1)}, bf16[128,256]{1,0:T(8,128)(2,1)S(1)}, bf16[128,256]{1,0:T(8,128)(2,1)S(1)}) custom-call(s32[1,2]{1,0:T(1,128)S(1)} %copy-done.4, f32[256,256]{1,0:T(8,128)S(1)} %get-tuple-element.49.vector, f32[256,256]{1,0:T(8,128)S(1)} %get-tuple-element.50.applied, bf16[2,128,256]{2,1,0:T(8,128)(2,1)S(1)} %bitcast.6, ...), custom_call_target="tpu_custom_call" | custom-call | flops 1677721600 | bytes 6553600 | tf_op jit(solution)/shard_map/second_step/pallas_call | solution.py:271
  120.6 2.0 %collective-permute-done.27.refs_1_ = bf16[128,256]{1,0:T(8,128)(2,1)S(1)} collective-permute-done((bf16[128,256]{1,0:T(8,128)(2,1)S(1)}, bf16[128,256]{1,0:T(8,128)(2,1)S(1)}, u32[]{:S(2)}, u32[]{:S(2)}) %collective-permute-start.27) | collective-permute-done | bytes 65568 | tf_op jit(solution)/shard_map/ppermute | solution.py:274
  122.7 2.6 %collective-permute-start.30 = (bf16[128,256]{1,0:T(8,128)(2,1)S(1)}, bf16[128,256]{1,0:T(8,128)(2,1)S(1)}, u32[]{:S(2)}, u32[]{:S(2)}) collective-permute-start(bf16[128,256]{1,0:T(8,128)(2,1)S(1)} %add.34.refs_0_), channel_id=1, source_target_pairs={{0,10},{1,11},{2,8},{3,9},{4,14},{5,15},{6,12},{7,13},{8,2},{9,3},... | collective-permute-start | bytes 196616 | tf_op jit(solution)/shard_map/ppermute | solution.py:274
  129.8 2.4 %collective-permute-done.28.refs_1_ = bf16[128,256]{1,0:T(8,128)(2,1)S(1)} collective-permute-done((bf16[128,256]{1,0:T(8,128)(2,1)S(1)}, bf16[128,256]{1,0:T(8,128)(2,1)S(1)}, u32[]{:S(2)}, u32[]{:S(2)}) %collective-permute-start.28) | collective-permute-done | bytes 65568 | tf_op jit(solution)/shard_map/ppermute | solution.py:274
  132.2 3.4 %all-gather.5 = bf16[256,256]{1,0:T(8,128)(2,1)S(1)} all-gather(bf16[128,256]{1,0:T(8,128)(2,1)S(1)} %add.35), channel_id=7, replica_groups={{0,1},{2,3},{4,5},{6,7},{8,9},{10,11},{12,13},{14,15},{16,17},{18,19},{..., dimensions={0}, use_global_device_ids=true | all-gather | bytes 196608 | tf_op jit(solution)/shard_map/all_gather | solution.py:294
  (78 shorter events, 45.3 us)
Async XLA Ops:
  3.8 61.2 %collective-permute-start.15 = (bf16[3776,256]{1,0:T(8,128)(2,1)S(1)}, bf16[3776,256]{1,0:T(8,128)(2,1)S(1)}, u32[]{:S(2)}, u32[]{:S(2)}) collective-permute-start(bf16[3776,256]{1,0:T(8,128)(2,1)S(1)} %pack.1), channel_id=1, source_target_pairs={{0,16},{16,32},{32,48},{48,64},{64,80},{80,96},{96,112},{112,128},... | collective-permute-start | bytes 5799944 | tf_op jit(solution)/shard_map/ppermute | solution.py:311
  10.5 1.9 %collective-permute-start = (bf16[128,256]{1,0:T(8,128)(2,1)S(1)}, bf16[128,256]{1,0:T(8,128)(2,1)S(1)}, u32[]{:S(2)}, u32[]{:S(2)}) collective-permute-start(bf16[128,256]{1,0:T(8,128)(2,1)S(1)} %get-tuple-element.32), channel_id=1, source_target_pairs={{0,1},{1,0},{2,3},{3,2},{4,5},{5,4},{6,7},{7,6},{8,9},{9,8},{10,11... | collective-permute-start | bytes 196616 | tf_op jit(solution)/shard_map/ppermute | solution.py:274
  12.4 3.8 %collective-permute-start.1 = (bf16[128,256]{1,0:T(8,128)(2,1)S(1)}, bf16[128,256]{1,0:T(8,128)(2,1)S(1)}, u32[]{:S(2)}, u32[]{:S(2)}) collective-permute-start(bf16[128,256]{1,0:T(8,128)(2,1)S(1)} %add.18.refs_0_), channel_id=1, source_target_pairs={{0,2},{1,3},{2,0},{3,1},{4,6},{5,7},{6,4},{7,5},{8,10},{9,11},{10,... | collective-permute-start | bytes 196616 | tf_op jit(solution)/shard_map/ppermute | solution.py:274
  16.2 7.7 %collective-permute-start.4 = (bf16[128,256]{1,0:T(8,128)(2,1)S(1)}, bf16[128,256]{1,0:T(8,128)(2,1)S(1)}, u32[]{:S(2)}, u32[]{:S(2)}) collective-permute-start(bf16[128,256]{1,0:T(8,128)(2,1)S(1)} %add.19.refs_0_), channel_id=1, source_target_pairs={{0,10},{1,11},{2,8},{3,9},{4,14},{5,15},{6,12},{7,13},{8,2},{9,3},... | collective-permute-start | bytes 196616 | tf_op jit(solution)/shard_map/ppermute | solution.py:274
  22.2 4.5 %collective-permute-start.3 = (bf16[128,256]{1,0:T(8,128)(2,1)S(1)}, bf16[128,256]{1,0:T(8,128)(2,1)S(1)}, u32[]{:S(2)}, u32[]{:S(2)}) collective-permute-start(bf16[128,256]{1,0:T(8,128)(2,1)S(1)} %add.19.refs_0_), channel_id=1, source_target_pairs={{0,14},{1,15},{2,4},{3,5},{4,2},{5,3},{6,8},{7,9},{8,6},{9,7},{10,... | collective-permute-start | bytes 196616 | tf_op jit(solution)/shard_map/ppermute | solution.py:274
  22.2 5.4 %collective-permute-start.2 = (bf16[128,256]{1,0:T(8,128)(2,1)S(1)}, bf16[128,256]{1,0:T(8,128)(2,1)S(1)}, u32[]{:S(2)}, u32[]{:S(2)}) collective-permute-start(bf16[128,256]{1,0:T(8,128)(2,1)S(1)} %add.19.refs_0_), channel_id=1, source_target_pairs={{0,12},{1,13},{2,6},{3,7},{4,0},{5,1},{6,10},{7,11},{8,4},{9,5},{1... | collective-permute-start | bytes 196616 | tf_op jit(solution)/shard_map/ppermute | solution.py:274
  34.1 1.3 collective-permute-start.5
  35.5 4.4 %collective-permute-start.6 = (bf16[128,256]{1,0:T(8,128)(2,1)S(1)}, bf16[128,256]{1,0:T(8,128)(2,1)S(1)}, u32[]{:S(2)}, u32[]{:S(2)}) collective-permute-start(bf16[128,256]{1,0:T(8,128)(2,1)S(1)} %add.21.refs_0_), channel_id=1, source_target_pairs={{0,2},{1,3},{2,0},{3,1},{4,6},{5,7},{6,4},{7,5},{8,10},{9,11},{10,... | collective-permute-start | bytes 196616 | tf_op jit(solution)/shard_map/ppermute | solution.py:274
  39.9 6.2 %collective-permute-start.9 = (bf16[128,256]{1,0:T(8,128)(2,1)S(1)}, bf16[128,256]{1,0:T(8,128)(2,1)S(1)}, u32[]{:S(2)}, u32[]{:S(2)}) collective-permute-start(bf16[128,256]{1,0:T(8,128)(2,1)S(1)} %add.22.refs_0_), channel_id=1, source_target_pairs={{0,10},{1,11},{2,8},{3,9},{4,14},{5,15},{6,12},{7,13},{8,2},{9,3},... | collective-permute-start | bytes 196616 | tf_op jit(solution)/shard_map/ppermute | solution.py:274
  42.3 5.3 %collective-permute-start.8 = (bf16[128,256]{1,0:T(8,128)(2,1)S(1)}, bf16[128,256]{1,0:T(8,128)(2,1)S(1)}, u32[]{:S(2)}, u32[]{:S(2)}) collective-permute-start(bf16[128,256]{1,0:T(8,128)(2,1)S(1)} %add.22.refs_0_), channel_id=1, source_target_pairs={{0,14},{1,15},{2,4},{3,5},{4,2},{5,3},{6,8},{7,9},{8,6},{9,7},{10,... | collective-permute-start | bytes 196616 | tf_op jit(solution)/shard_map/ppermute | solution.py:274
  43.8 5.0 %collective-permute-start.7 = (bf16[128,256]{1,0:T(8,128)(2,1)S(1)}, bf16[128,256]{1,0:T(8,128)(2,1)S(1)}, u32[]{:S(2)}, u32[]{:S(2)}) collective-permute-start(bf16[128,256]{1,0:T(8,128)(2,1)S(1)} %add.22.refs_0_), channel_id=1, source_target_pairs={{0,12},{1,13},{2,6},{3,7},{4,0},{5,1},{6,10},{7,11},{8,4},{9,5},{1... | collective-permute-start | bytes 196616 | tf_op jit(solution)/shard_map/ppermute | solution.py:274
  53.0 12.0 %copy-start.3 = (bf16[1,256,256]{2,1,0:T(8,128)(2,1)S(1)}, bf16[1,256,256]{2,1,0:T(8,128)(2,1)}, u32[]{:S(2)}) copy-start(bf16[1,256,256]{2,1,0:T(8,128)(2,1)} %start.3) | copy-start | bytes 393220
  55.6 1.3 collective-permute-start.10
  57.0 3.2 %collective-permute-start.11 = (bf16[128,256]{1,0:T(8,128)(2,1)S(1)}, bf16[128,256]{1,0:T(8,128)(2,1)S(1)}, u32[]{:S(2)}, u32[]{:S(2)}) collective-permute-start(bf16[128,256]{1,0:T(8,128)(2,1)S(1)} %add.24.refs_0_), channel_id=1, source_target_pairs={{0,2},{1,3},{2,0},{3,1},{4,6},{5,7},{6,4},{7,5},{8,10},{9,11},{10,... | collective-permute-start | bytes 196616 | tf_op jit(solution)/shard_map/ppermute | solution.py:274
  60.2 6.4 %collective-permute-start.14 = (bf16[128,256]{1,0:T(8,128)(2,1)S(1)}, bf16[128,256]{1,0:T(8,128)(2,1)S(1)}, u32[]{:S(2)}, u32[]{:S(2)}) collective-permute-start(bf16[128,256]{1,0:T(8,128)(2,1)S(1)} %add.25.refs_0_), channel_id=1, source_target_pairs={{0,10},{1,11},{2,8},{3,9},{4,14},{5,15},{6,12},{7,13},{8,2},{9,3},... | collective-permute-start | bytes 196616 | tf_op jit(solution)/shard_map/ppermute | solution.py:274
  62.7 4.6 %collective-permute-start.13 = (bf16[128,256]{1,0:T(8,128)(2,1)S(1)}, bf16[128,256]{1,0:T(8,128)(2,1)S(1)}, u32[]{:S(2)}, u32[]{:S(2)}) collective-permute-start(bf16[128,256]{1,0:T(8,128)(2,1)S(1)} %add.25.refs_0_), channel_id=1, source_target_pairs={{0,14},{1,15},{2,4},{3,5},{4,2},{5,3},{6,8},{7,9},{8,6},{9,7},{10,... | collective-permute-start | bytes 196616 | tf_op jit(solution)/shard_map/ppermute | solution.py:274
  64.1 5.5 %collective-permute-start.12 = (bf16[128,256]{1,0:T(8,128)(2,1)S(1)}, bf16[128,256]{1,0:T(8,128)(2,1)S(1)}, u32[]{:S(2)}, u32[]{:S(2)}) collective-permute-start(bf16[128,256]{1,0:T(8,128)(2,1)S(1)} %add.25.refs_0_), channel_id=1, source_target_pairs={{0,12},{1,13},{2,6},{3,7},{4,0},{5,1},{6,10},{7,11},{8,4},{9,5},{1... | collective-permute-start | bytes 196616 | tf_op jit(solution)/shard_map/ppermute | solution.py:274
  76.6 1.3 collective-permute-start.16
  77.9 3.2 %collective-permute-start.17 = (bf16[128,256]{1,0:T(8,128)(2,1)S(1)}, bf16[128,256]{1,0:T(8,128)(2,1)S(1)}, u32[]{:S(2)}, u32[]{:S(2)}) collective-permute-start(bf16[128,256]{1,0:T(8,128)(2,1)S(1)} %add.27.refs_0_), channel_id=1, source_target_pairs={{0,2},{1,3},{2,0},{3,1},{4,6},{5,7},{6,4},{7,5},{8,10},{9,11},{10,... | collective-permute-start | bytes 196616 | tf_op jit(solution)/shard_map/ppermute | solution.py:274
  81.1 6.3 %collective-permute-start.20 = (bf16[128,256]{1,0:T(8,128)(2,1)S(1)}, bf16[128,256]{1,0:T(8,128)(2,1)S(1)}, u32[]{:S(2)}, u32[]{:S(2)}) collective-permute-start(bf16[128,256]{1,0:T(8,128)(2,1)S(1)} %add.28.refs_0_), channel_id=1, source_target_pairs={{0,10},{1,11},{2,8},{3,9},{4,14},{5,15},{6,12},{7,13},{8,2},{9,3},... | collective-permute-start | bytes 196616 | tf_op jit(solution)/shard_map/ppermute | solution.py:274
  83.7 4.5 %collective-permute-start.19 = (bf16[128,256]{1,0:T(8,128)(2,1)S(1)}, bf16[128,256]{1,0:T(8,128)(2,1)S(1)}, u32[]{:S(2)}, u32[]{:S(2)}) collective-permute-start(bf16[128,256]{1,0:T(8,128)(2,1)S(1)} %add.28.refs_0_), channel_id=1, source_target_pairs={{0,14},{1,15},{2,4},{3,5},{4,2},{5,3},{6,8},{7,9},{8,6},{9,7},{10,... | collective-permute-start | bytes 196616 | tf_op jit(solution)/shard_map/ppermute | solution.py:274
  85.1 5.5 %collective-permute-start.18 = (bf16[128,256]{1,0:T(8,128)(2,1)S(1)}, bf16[128,256]{1,0:T(8,128)(2,1)S(1)}, u32[]{:S(2)}, u32[]{:S(2)}) collective-permute-start(bf16[128,256]{1,0:T(8,128)(2,1)S(1)} %add.28.refs_0_), channel_id=1, source_target_pairs={{0,12},{1,13},{2,6},{3,7},{4,0},{5,1},{6,10},{7,11},{8,4},{9,5},{1... | collective-permute-start | bytes 196616 | tf_op jit(solution)/shard_map/ppermute | solution.py:274
  97.3 1.3 collective-permute-start.21
  98.6 3.2 %collective-permute-start.22 = (bf16[128,256]{1,0:T(8,128)(2,1)S(1)}, bf16[128,256]{1,0:T(8,128)(2,1)S(1)}, u32[]{:S(2)}, u32[]{:S(2)}) collective-permute-start(bf16[128,256]{1,0:T(8,128)(2,1)S(1)} %add.30.refs_0_), channel_id=1, source_target_pairs={{0,2},{1,3},{2,0},{3,1},{4,6},{5,7},{6,4},{7,5},{8,10},{9,11},{10,... | collective-permute-start | bytes 196616 | tf_op jit(solution)/shard_map/ppermute | solution.py:274
  101.9 6.3 %collective-permute-start.25 = (bf16[128,256]{1,0:T(8,128)(2,1)S(1)}, bf16[128,256]{1,0:T(8,128)(2,1)S(1)}, u32[]{:S(2)}, u32[]{:S(2)}) collective-permute-start(bf16[128,256]{1,0:T(8,128)(2,1)S(1)} %add.31.refs_0_), channel_id=1, source_target_pairs={{0,10},{1,11},{2,8},{3,9},{4,14},{5,15},{6,12},{7,13},{8,2},{9,3},... | collective-permute-start | bytes 196616 | tf_op jit(solution)/shard_map/ppermute | solution.py:274
  104.5 4.5 %collective-permute-start.24 = (bf16[128,256]{1,0:T(8,128)(2,1)S(1)}, bf16[128,256]{1,0:T(8,128)(2,1)S(1)}, u32[]{:S(2)}, u32[]{:S(2)}) collective-permute-start(bf16[128,256]{1,0:T(8,128)(2,1)S(1)} %add.31.refs_0_), channel_id=1, source_target_pairs={{0,14},{1,15},{2,4},{3,5},{4,2},{5,3},{6,8},{7,9},{8,6},{9,7},{10,... | collective-permute-start | bytes 196616 | tf_op jit(solution)/shard_map/ppermute | solution.py:274
  105.9 5.5 %collective-permute-start.23 = (bf16[128,256]{1,0:T(8,128)(2,1)S(1)}, bf16[128,256]{1,0:T(8,128)(2,1)S(1)}, u32[]{:S(2)}, u32[]{:S(2)}) collective-permute-start(bf16[128,256]{1,0:T(8,128)(2,1)S(1)} %add.31.refs_0_), channel_id=1, source_target_pairs={{0,12},{1,13},{2,6},{3,7},{4,0},{5,1},{6,10},{7,11},{8,4},{9,5},{1... | collective-permute-start | bytes 196616 | tf_op jit(solution)/shard_map/ppermute | solution.py:274
  118.1 1.3 collective-permute-start.26
  119.4 3.2 %collective-permute-start.27 = (bf16[128,256]{1,0:T(8,128)(2,1)S(1)}, bf16[128,256]{1,0:T(8,128)(2,1)S(1)}, u32[]{:S(2)}, u32[]{:S(2)}) collective-permute-start(bf16[128,256]{1,0:T(8,128)(2,1)S(1)} %add.33.refs_0_), channel_id=1, source_target_pairs={{0,2},{1,3},{2,0},{3,1},{4,6},{5,7},{6,4},{7,5},{8,10},{9,11},{10,... | collective-permute-start | bytes 196616 | tf_op jit(solution)/shard_map/ppermute | solution.py:274
  122.7 6.3 %collective-permute-start.30 = (bf16[128,256]{1,0:T(8,128)(2,1)S(1)}, bf16[128,256]{1,0:T(8,128)(2,1)S(1)}, u32[]{:S(2)}, u32[]{:S(2)}) collective-permute-start(bf16[128,256]{1,0:T(8,128)(2,1)S(1)} %add.34.refs_0_), channel_id=1, source_target_pairs={{0,10},{1,11},{2,8},{3,9},{4,14},{5,15},{6,12},{7,13},{8,2},{9,3},... | collective-permute-start | bytes 196616 | tf_op jit(solution)/shard_map/ppermute | solution.py:274
  125.3 4.5 %collective-permute-start.29 = (bf16[128,256]{1,0:T(8,128)(2,1)S(1)}, bf16[128,256]{1,0:T(8,128)(2,1)S(1)}, u32[]{:S(2)}, u32[]{:S(2)}) collective-permute-start(bf16[128,256]{1,0:T(8,128)(2,1)S(1)} %add.34.refs_0_), channel_id=1, source_target_pairs={{0,14},{1,15},{2,4},{3,5},{4,2},{5,3},{6,8},{7,9},{8,6},{9,7},{10,... | collective-permute-start | bytes 196616 | tf_op jit(solution)/shard_map/ppermute | solution.py:274
  126.7 5.5 %collective-permute-start.28 = (bf16[128,256]{1,0:T(8,128)(2,1)S(1)}, bf16[128,256]{1,0:T(8,128)(2,1)S(1)}, u32[]{:S(2)}, u32[]{:S(2)}) collective-permute-start(bf16[128,256]{1,0:T(8,128)(2,1)S(1)} %add.34.refs_0_), channel_id=1, source_target_pairs={{0,12},{1,13},{2,6},{3,7},{4,0},{5,1},{6,10},{7,11},{8,4},{9,5},{1... | collective-permute-start | bytes 196616 | tf_op jit(solution)/shard_map/ppermute | solution.py:274
  (6 other events, 21.7 us)
